TPU v7x, 128 devices: a whole 4x4x4 slice. The times are simulated.
128 devices in a mesh: ctx: 32 (over z, y, core), head: 4 (over x).
Axes of the slice: x: 4, y: 4, z: 4, core: 2. Of those that a mesh axis runs over, the one named last changes fastest.
Arguments:
- ctx_query: bfloat16 [32768, 4096], P('ctx', 'head'), may hold values from -30 to 30
- ctx_key: bfloat16 [32768, 1024], P('ctx', 'head'), may hold values from -13.5625 to 13.5625
- ctx_value: bfloat16 [32768, 1024], P('ctx', 'head'), may hold values from -6 to 6
- quest_query: bfloat16 [256, 4096], P(None, 'head'), may hold values from -30 to 30
- quest_key: bfloat16 [256, 1024], P(None, 'head'), may hold values from -13.5625 to 13.5625
- quest_value: bfloat16 [256, 1024], P(None, 'head'), may hold values from -6 to 6
- quest_order: int32 [256], replicated, may hold values from 0 to 255, each once
- out_weight: bfloat16 [4096, 4096], P('head'), may hold values from -0.09375 to 0.09375
Outputs:
- ctx_out: bfloat16 [32768, 4096], P('ctx', 'head')
- answer: bfloat16 [256, 4096], P('ctx', 'head')
Inputs may be any that keep to these rules, and one draw needn't show every extreme that they name: `quest_order`: each of 0 to 255 appears once.
All inputs are finite; a program needn't handle non-finite values.
Results may differ from a plain program's by a relative error of at most 0.005.
Values may be sent and summed in bfloat16 or wider, within the bound.
No kernel may reach another device: no remote copies, remote signals or barrier semaphores. Data moves between devices by JAX's collectives and lax.ppermute only.
A program may use at most 256 MiB of HBM per device.

v0:
```python
import math

import jax
import jax.numpy as jnp
from jax import lax
from jax.sharding import PartitionSpec as P

HEAD_DIM = 128


def from_root(block, axis, holder):
    block = jnp.where(lax.axis_index(axis) == holder, block, jnp.zeros_like(block))
    return lax.psum(block, axis)


def attend_block(queries, cached_keys, cached_values, allowed):
    row_count = queries.shape[0]
    kv_count = cached_keys.shape[1] // HEAD_DIM
    group_size = queries.shape[1] // cached_keys.shape[1]
    query_heads = queries.reshape(row_count, kv_count, group_size, HEAD_DIM)
    key_heads = cached_keys.reshape(-1, kv_count, HEAD_DIM)
    value_heads = cached_values.reshape(-1, kv_count, HEAD_DIM)
    scores = jnp.einsum(
        "rkgd,ckd->kgrc", query_heads, key_heads, preferred_element_type=jnp.float32
    ) / math.sqrt(HEAD_DIM)
    scores = jnp.where(allowed, scores, -jnp.inf)
    maxima = jnp.max(scores, axis=-1)
    weights = jnp.exp(scores - maxima[..., None])
    totals = jnp.sum(weights, axis=-1)
    weighted = jnp.einsum(
        "kgrc,ckd->rkgd",
        weights.astype(jnp.bfloat16),
        value_heads,
        preferred_element_type=jnp.float32,
    )
    return (
        jnp.transpose(maxima, (2, 0, 1)).reshape(row_count, -1),
        jnp.transpose(totals, (2, 0, 1)).reshape(row_count, -1),
        weighted.reshape(row_count, -1),
    )


def per_device(
    ctx_query, ctx_key, ctx_value, quest_query, quest_key, quest_value, quest_order, out_weight
):
    row_count = ctx_query.shape[0]
    kv_width = ctx_key.shape[1]
    kv_count = kv_width // HEAD_DIM
    query_width = ctx_query.shape[1] // kv_count
    anchor = from_root(jnp.stack([ctx_key, ctx_value]), "ctx", 0)
    not_root = lax.axis_index("ctx") > 0
    row_ids = lax.broadcasted_iota(jnp.int32, (row_count, row_count), 0)
    col_ids = lax.broadcasted_iota(jnp.int32, (row_count, row_count), 1)
    allowed = jnp.concatenate(
        [jnp.broadcast_to(not_root, (row_count, row_count)), col_ids <= row_ids], axis=1
    )
    all_keys = jnp.concatenate([anchor[0], ctx_key], axis=0)
    all_values = jnp.concatenate([anchor[1], ctx_value], axis=0)
    head_outputs = []
    for kv_head in range(kv_count):
        query_cols = ctx_query[:, kv_head * query_width : (kv_head + 1) * query_width]
        key_cols = all_keys[:, kv_head * HEAD_DIM : (kv_head + 1) * HEAD_DIM]
        value_cols = all_values[:, kv_head * HEAD_DIM : (kv_head + 1) * HEAD_DIM]
        maxima, totals, weighted = attend_block(query_cols, key_cols, value_cols, allowed)
        head_outputs.append(weighted / jnp.repeat(totals, HEAD_DIM, axis=1))
    ctx_out = jnp.concatenate(head_outputs, axis=1).astype(jnp.bfloat16)
    block_max, block_total, block_sum = attend_block(quest_query, ctx_key, ctx_value, True)
    order_allowed = quest_order[None, :] <= quest_order[:, None]
    self_max, self_total, self_sum = attend_block(
        quest_query, quest_key, quest_value, order_allowed
    )
    row_share = quest_query.shape[0] // lax.axis_size("ctx")
    first_row = lax.axis_index("ctx") * row_share
    ctx_peak = lax.pmax(block_max, "ctx")
    peak = jnp.maximum(ctx_peak, self_max)
    block_scale = jnp.exp(block_max - peak)
    summed = (
        lax.psum_scatter(block_total * block_scale, "ctx", scatter_dimension=0, tiled=True),
        lax.psum_scatter(
            block_sum * jnp.repeat(block_scale, HEAD_DIM, axis=1),
            "ctx",
            scatter_dimension=0,
            tiled=True,
        ),
    )
    own_peak = lax.dynamic_slice_in_dim(peak, first_row, row_share, 0)
    self_scale = jnp.exp(lax.dynamic_slice_in_dim(self_max, first_row, row_share, 0) - own_peak)
    totals = summed[0] + lax.dynamic_slice_in_dim(self_total, first_row, row_share, 0) * self_scale
    combined = summed[1] + lax.dynamic_slice_in_dim(self_sum, first_row, row_share, 0) * jnp.repeat(
        self_scale, HEAD_DIM, axis=1
    )
    attended = (combined / jnp.repeat(totals, HEAD_DIM, axis=1)).astype(jnp.bfloat16)
    projected = jnp.dot(attended, out_weight, preferred_element_type=jnp.float32)
    answer = lax.psum_scatter(projected, "head", scatter_dimension=1, tiled=True).astype(
        jnp.bfloat16
    )
    return (ctx_out, answer)


def solution(mesh):
    in_specs = (
        P("ctx", "head"),
        P("ctx", "head"),
        P("ctx", "head"),
        P(None, "head"),
        P(None, "head"),
        P(None, "head"),
        P(),
        P("head", None),
    )
    out_specs = (P("ctx", "head"), P("ctx", "head"))
    return jax.shard_map(
        per_device, mesh=mesh, in_specs=in_specs, out_specs=out_specs, check_vma=False
    )
```

profile of v0, /device:TPU:1, one launch (start us, length us, event | category | flops | bytes accessed | tf_op | source)
XLA Modules:
  0.0 306.4 jit_solution(13450041607493599967)
XLA Ops:
  7.2 2.3 maximum_select_fusion
  9.6 2.0 reshape.127
  11.5 1.2 copy.78
  14.6 1.4 reshape.128
  16.5 5.5 %bitcast_reduce_fusion = (f32[2,4,256]{2,1,0:T(4,128)S(1)}, f32[2,1024,256,4]{2,1,3,0:T(8,128)}) fusion(bf16[256,2,4,128]{3,2,1,0:T(4,128)(2,1)S(1)} %reshape.128, bf16[1024,2,128,1]{2,1,0,3:T(2,128)(2,1)} %bitcast.159), kind=kOutput, calls=%fused_computation.17 | convolution fusion | flops 541063168 | bytes 9445376 | tf_op jit(solution)/shard_map/rkgd,ckd->kgrc/dot_general | solution.py:23
  22.1 66.2 %pmax.7 = f32[256,8]{0,1:T(8,128)S(1)} all-reduce(f32[256,8]{0,1:T(8,128)S(1)} %reshape.131), channel_id=1, replica_groups=mesh['ctx'=32,'head'=4] {'ctx'}, use_global_device_ids=true, to_apply=%region_6.7 | all-reduce | flops 2048 | bytes 16384 | tf_op jit(solution)/shard_map/pmax | solution.py:74
  88.3 4.8 %fusion.15 = f32[2,4,256]{2,1,0:T(4,128)S(1)} fusion(f32[2,1024,256,4]{2,1,3,0:T(8,128)} %get-tuple-element.17, f32[2,4,256]{2,1,0:T(4,128)S(1)} %get-tuple-element.16), kind=kLoop, calls=%fused_computation.19 | loop fusion | flops 6289408 | bytes 8404992 | tf_op jit(solution)/shard_map/reduce_sum | solution.py:29
  93.1 5.1 %fusion.17 = f32[2,4,256,128]{2,3,1,0:T(8,128)S(1)} fusion(bf16[1024,2,128,1]{0,2,3,1:T(8,128)(2,1)S(1)} %bitcast.156, f32[2,1024,256,4]{2,1,3,0:T(8,128)} %get-tuple-element.17, f32[2,4,256]{2,1,0:T(4,128)S(1)} %get-tuple-element.16), kind=kOutput, calls=%fused_computation.21 | convolution fusion | flops 543162368 | bytes 9969664 | tf_op jit(solution)/shard_map/kgrc,ckd->rkgd/dot_general | solution.py:30
  98.3 1.3 copy.82
  100.4 1.5 fusion.25
  101.9 1.7 fusion.59
  103.6 1.3 copy.86
  105.0 1.3 copy.87
  106.3 68.1 %all-reduce.1 = f32[256,8]{0,1:T(8,128)S(1)} all-reduce(f32[256,8]{0,1:T(8,128)S(1)} %get-tuple-element.6), channel_id=3, replica_groups=mesh['ctx'=32,'head'=4] {'ctx'}, use_global_device_ids=true, to_apply=%region_10.11.clone | all-reduce | flops 2048 | bytes 16384
  176.3 1.9 slice_bitcast_fusion.1
  178.3 15.4 %fusion.4 = (f32[4,1024]{1,0:T(4,128)S(1)}, f32[2048,1024,4]{1,0,2:T(8,128)}) fusion(pred[1024,2048]{0,1:T(8,128)(4,1)S(1)} %concatenate.14, bf16[1024,4,128]{0,2,1:T(8,128)(2,1)} %bitcast.161, bf16[1024,256]{1,0:T(8,128)(2,1)S(1)} %get-tuple-element.12, bf16[1024,256]{1,0:T(8,128)(2,1)} %param.9), kind=kOutput, calls=%fused_computation.8 | convolution fusion | flops 2173693952 | bytes 37765120 | tf_op jit(solution)/shard_map/rkgd,ckd->kgrc/dot_general | solution.py:23
  193.8 17.2 %fusion.8 = f32[128,4,1024]{2,0,1:T(8,128)} fusion(f32[2048,1024,4]{1,0,2:T(8,128)} %get-tuple-element.14, f32[4,1024]{1,0:T(4,128)S(1)} %get-tuple-element.13, pred[1024,2048]{0,1:T(8,128)(4,1)S(1)} %concatenate.14, bf16[1024,256]{1,0:T(8,128)(2,1)S(1)} %get-tuple-element.11, bf16[1024,256]{1,0:T(8,128)(2,1)S(1)} %copy-done.3), kind=kOutput, calls=%fused_computation.12 | convolution fusion | flops 2182086656 | bytes 38813696 | tf_op jit(solution)/shard_map/kgrc,ckd->rkgd/dot_general | solution.py:30
  210.9 25.8 %fusion = (f32[4,1024]{1,0:T(4,128)S(1)}, f32[4,1024]{1,0:T(4,128)S(1)}, f32[2048,1024,4]{1,0,2:T(8,128)}) fusion(f32[2048,1024,4]{1,0,2:T(8,128)} %get-tuple-element.14, f32[4,1024]{1,0:T(4,128)S(1)} %get-tuple-element.13, pred[1024,2048]{0,1:T(8,128)(4,1)S(1)} %concatenate.14, bf16[1024,4,128]{0,2,1:T(8,128)(2,1)S(1)} %bitcast.160, ...), kind=kOutput, calls=%fused_computation.4 | convolution fusion | flops 2207244288 | bytes 71352320 | tf_op jit(solution)/shard_map/rkgd,ckd->kgrc/dot_general | solution.py:23
  236.8 1.9 copy.47
  238.7 17.3 %fusion.10 = f32[128,4,1024]{2,0,1:T(8,128)} fusion(f32[2048,1024,4]{1,0,2:T(8,128)} %get-tuple-element.15, f32[4,1024]{1,0:T(4,128)S(1)} %get-tuple-element.3, pred[1024,2048]{0,1:T(8,128)(4,1)} %copy-done, bf16[1024,256]{1,0:T(8,128)(2,1)S(1)} %copy-done.3, bf16[1024,256]{1,0:T(8,128)(2,1)S(1)} %get-tuple-element.11), kind=kOutput, calls=%fused_computation.13 | convolution fusion | flops 2182086656 | bytes 38813696 | tf_op jit(solution)/shard_map/kgrc,ckd->rkgd/dot_general | solution.py:30
  256.0 2.9 copy.53
  258.9 14.5 %fusion.2 = f32[4,1024]{1,0:T(4,128)S(1)} fusion(f32[2048,1024,4]{1,0,2:T(8,128)} %get-tuple-element.15, f32[4,1024]{1,0:T(4,128)S(1)} %get-tuple-element.3, pred[1024,2048]{0,1:T(8,128)(4,1)} %copy-done), kind=kLoop, calls=%fused_computation.6 | loop fusion | flops 33550336 | bytes 35684352 | tf_op jit(solution)/shard_map/reduce_sum | solution.py:29
  273.5 1.0 copy.52
  275.5 1.8 copy.83
  277.3 1.2 fusion.42
  278.6 5.4 %fusion.61 = f32[8,4096]{1,0:T(8,128)} fusion(bf16[8,1024]{0,1:T(8,128)(2,1)S(1)} %fusion.42, bf16[1024,4096]{1,0:T(8,128)(2,1)} %param.15), kind=kOutput, calls=%fused_computation.81 | convolution fusion | flops 67108864 | bytes 8536064 | tf_op jit(solution)/shard_map/dot_general | solution.py:93
  284.0 1.2 broadcast_in_dim.48
  285.2 1.2 broadcast_in_dim.49
  286.4 2.5 fusion.21
  288.9 1.6 pad_maximum_fusion
  290.5 8.0 %reduce-scatter.6.cloned.1.call-done = f32[8,1024]{1,0:T(8,128)} async-done(((f32[8,4096]{1,0:T(8,128)}), f32[8,1024]{1,0:T(8,128)}) %reduce-scatter.6.cloned.1.call-update) | async-done | bytes 32784 | tf_op jit(solution)/shard_map/reduce_scatter | solution.py:94
  298.5 1.4 convert_element_type.24
  (44 shorter events, 5.7 us)
Async XLA Ops:
  7.2 169.2 %all-reduce.4.cloned.1.call-start = ((), (), s32[]{:S(2)}) async-start(), calls=%async_computation.2 | async-start | bytes 2097152 | tf_op jit(solution)/shard_map/psum | solution.py:13
  9.5 266.0 %reduce-scatter.8.cloned.1.call-start = ((), (), s32[]{:S(2)}) async-start(), calls=%async_computation.4 | async-start | bytes 1081344
  93.1 6.9 %copy-start.8 = (bf16[256,256]{1,0:T(8,128)(2,1)S(1)}, bf16[256,256]{1,0:T(8,128)(2,1)}, u32[]{:S(2)}) copy-start(bf16[256,256]{1,0:T(8,128)(2,1)} %param.13) | copy-start | bytes 393220
  99.6 74.8 %copy-start.9 = (u32[128]{0:T(128)S(1)}, u32[128]{0:T(128)}, u32[]{:S(2)}) copy-start(u32[128]{0:T(128)} %constant.31) | copy-start | bytes 1540
  99.6 198.9 %reduce-scatter.6.cloned.1.call-start = ((), (), s32[]{:S(2)}) async-start(), calls=%async_computation.3 | async-start | bytes 163840 | tf_op jit(solution)/shard_map/reduce_scatter | solution.py:94
  176.2 34.7 %copy-start = (pred[1024,2048]{0,1:T(8,128)(4,1)}, pred[1024,2048]{0,1:T(8,128)(4,1)S(1)}, u32[]{:S(2)}) copy-start(pred[1024,2048]{0,1:T(8,128)(4,1)S(1)} %concatenate.14) | copy-start | bytes 6291460
  178.3 15.4 %copy-start.7 = (bf16[1024,256]{1,0:T(8,128)(2,1)}, bf16[1024,256]{1,0:T(8,128)(2,1)S(1)}, u32[]{:S(2)}) copy-start(bf16[1024,256]{1,0:T(8,128)(2,1)S(1)} %get-tuple-element.12) | copy-start | bytes 1572868
  178.3 15.4 %copy-start.3 = (bf16[1024,256]{1,0:T(8,128)(2,1)S(1)}, bf16[1024,256]{1,0:T(8,128)(2,1)}, u32[]{:S(2)}) copy-start(bf16[1024,256]{1,0:T(8,128)(2,1)} %param.10) | copy-start | bytes 1572868
  193.7 17.2 %copy-start.2 = (bf16[1024,256]{1,0:T(8,128)(2,1)S(1)}, bf16[1024,256]{1,0:T(8,128)(2,1)}, u32[]{:S(2)}) copy-start(bf16[1024,256]{1,0:T(8,128)(2,1)} %param.9) | copy-start | bytes 1572868
  193.7 17.2 %copy-start.6 = (bf16[1024,512]{0,1:T(8,128)(2,1)S(1)}, bf16[1024,512]{0,1:T(8,128)(2,1)}, u32[]{:S(2)}) copy-start(bf16[1024,512]{0,1:T(8,128)(2,1)} %copy.87) | copy-start | bytes 3145732
  258.9 18.4 %copy-start.1 = (f32[2,4,256,128]{2,3,1,0:T(8,128)S(1)}, f32[2,4,256,128]{2,3,1,0:T(8,128)}, u32[]{:S(2)}) copy-start(f32[2,4,256,128]{2,3,1,0:T(8,128)} %fusion.25) | copy-start | bytes 3145732
  278.5 5.4 %copy-start.5 = (f32[1024,4]{1,0:T(8,128)S(1)}, f32[1024,4]{1,0:T(8,128)}, u32[]{:S(2)}) copy-start(f32[1024,4]{1,0:T(8,128)} %copy.46) | copy-start | bytes 49156
  278.5 6.7 %copy-start.4 = (f32[1024,4]{1,0:T(8,128)S(1)}, f32[1024,4]{1,0:T(8,128)}, u32[]{:S(2)}) copy-start(f32[1024,4]{1,0:T(8,128)} %copy.52) | copy-start | bytes 49156
Sparse Core Ops, SparseCore 0:
  11.2 108.1 all-reduce.3
  123.4 75.8 reduce-scatter.7
  284.1 14.3 reduce-scatter.5
where the time goes:
time: 309 us; the launch traced here: 306 us
  blocking collectives  134 us (43%)
  matrix products  93.7 us (30%)
  other arithmetic  29.9 us (10%)
  local copies, waits for them, and re-layouts  25.7 us (8%)
  between operations  14.7 us (5%)
  waiting for transfers between devices  8.01 us (3%)
    unnamed x1, blocking collectives  68.1 us
    pmax x1, blocking collectives, per_device(): ctx_peak = lax.pmax(block_max, 'ctx')  66.2 us
    dot_general x4, matrix products, attend_block(): jnp.einsum('rkgd,ckd->kgrc', query_heads, key_heads, preferred_element_ty...  47.3 us
    dot_general x4, matrix products, attend_block(): jnp.einsum('kgrc,ckd->rkgd', weights.astype(jnp.bfloat16), value_heads, p...  41 us
    reduce_sum x3, other arithmetic, attend_block(): totals = jnp.sum(weights, axis=-1)  19.6 us
    reduce_scatter x1, waiting for transfers between devices, per_device(): lax.psum_scatter(projected, 'head', scatter_dimension=1, tiled=True)  7.96 us
    unnamed x25, local copies, waits for them, and re-layouts  6.39 us
  transfers between devices with their start and end apart: 3, of which 1 were waited for; matrix products, arithmetic and copies ran while one was open for 45% of the time, Pallas kernels for 0%

commit v1 on v0

v1 whole, which is shorter than its diff:
```python
import math

import jax
import jax.numpy as jnp
from jax import lax
from jax.experimental import pallas as pl
from jax.experimental.pallas import tpu as pltpu
from jax.sharding import PartitionSpec as P

HEAD_DIM = 128
BLOCK = 1024
TILE = 256
QROWS = 256
GROUP = 4
HEADS = 8
EXTRA = 128
SCALE = math.log2(math.e) / math.sqrt(HEAD_DIM)
F32 = jnp.float32
BF16 = jnp.bfloat16
VMEM_LIMIT = 48 * 1024 * 1024


def scores_of(queries, keys):
    return lax.dot_general(queries, keys, (((1,), (1,)), ((), ())), preferred_element_type=F32)


def weigh(scores):
    maxima = jnp.max(scores, axis=-1, keepdims=True)
    weights = jnp.exp2((scores - maxima) * SCALE)
    return maxima, weights, jnp.sum(weights, axis=-1, keepdims=True)


def times_values(weights, values):
    return jnp.dot(weights.astype(BF16), values, preferred_element_type=F32)


def head_cols(head):
    return slice(head * HEAD_DIM, (head + 1) * HEAD_DIM)


def question_kernel(query_ref, key_ref, value_ref, out_ref, lse_ref):
    lse_ref[...] = jnp.zeros_like(lse_ref)
    for head in range(HEADS):
        kv = head // GROUP
        scores = scores_of(query_ref[:, head_cols(head)], key_ref[:, head_cols(kv)])
        maxima, weights, totals = weigh(scores)
        summed = times_values(weights, value_ref[:, head_cols(kv)])
        out_ref[:, head_cols(head)] = (summed / totals).astype(BF16)
        rest = maxima * SCALE + jnp.log2(totals)
        for part in range(3):
            term = rest.astype(BF16).astype(F32)
            at = part * HEADS + head
            lse_ref[:, at : at + 1] = term
            rest = rest - term
    out_ref[:, HEADS * HEAD_DIM :] = lse_ref[...].astype(BF16)


def question_part(quest_query, ctx_key, ctx_value):
    rows, width = quest_query.shape
    return pl.pallas_call(
        question_kernel,
        out_shape=jax.ShapeDtypeStruct((rows, width + EXTRA), BF16),
        scratch_shapes=[pltpu.VMEM((rows, EXTRA), F32)],
        compiler_params=pltpu.CompilerParams(vmem_limit_bytes=VMEM_LIMIT),
        cost_estimate=pl.CostEstimate(
            flops=4 * rows * width * BLOCK, bytes_accessed=2 << 20, transcendentals=rows * HEADS * BLOCK
        ),
        name="question_block",
    )(quest_query, ctx_key, ctx_value)


def self_kernel(place_ref, order_ref, query_ref, key_ref, value_ref, order_row_ref, out_ref, lse_ref):
    first = (place_ref[0] // 2) * 16
    row_ids = lax.broadcasted_iota(jnp.int32, (16, QROWS), 0)
    row_order = jnp.zeros((16, QROWS), jnp.int32)
    for row in range(16):
        row_order = jnp.where(row_ids == row, order_ref[first + row], row_order)
    allowed = order_row_ref[...] <= row_order
    upper = place_ref[0] % 2 == 1
    lane = lax.broadcasted_iota(jnp.int32, (8, EXTRA), 1)
    lse = jnp.zeros((8, EXTRA), F32)
    for head in range(HEADS):
        kv = head // GROUP
        scores = scores_of(query_ref[:, head_cols(head)], key_ref[:, head_cols(kv)])
        scores = jnp.where(allowed, scores, -jnp.inf)
        maxima, weights, totals = weigh(scores)
        summed = times_values(weights, value_ref[:, head_cols(kv)]) / totals
        row_lse = maxima * SCALE + jnp.log2(totals)
        out_ref[:, head_cols(head)] = jnp.where(upper, summed[8:], summed[:8])
        lse = jnp.where(lane == head, jnp.where(upper, row_lse[8:], row_lse[:8]), lse)
    lse_ref[...] = lse


def self_part(place, quest_query, quest_key, quest_value, quest_order):
    width = quest_query.shape[1]
    kv_width = quest_key.shape[1]
    whole = lambda i, place, order: (0, 0)
    return pl.pallas_call(
        self_kernel,
        out_shape=(
            jax.ShapeDtypeStruct((8, width), F32),
            jax.ShapeDtypeStruct((8, EXTRA), F32),
        ),
        grid_spec=pltpu.PrefetchScalarGridSpec(
            num_scalar_prefetch=2,
            grid=(1,),
            in_specs=[
                pl.BlockSpec((16, width), lambda i, place, order: (place[0] // 2, 0)),
                pl.BlockSpec((QROWS, kv_width), whole),
                pl.BlockSpec((QROWS, kv_width), whole),
                pl.BlockSpec((1, QROWS), whole),
            ],
            out_specs=(pl.BlockSpec((8, width), whole), pl.BlockSpec((8, EXTRA), whole)),
        ),
        cost_estimate=pl.CostEstimate(flops=1 << 28, bytes_accessed=1 << 19, transcendentals=1 << 15),
        name="question_self",
    )(place, quest_order, quest_query, quest_key, quest_value, quest_order.reshape(1, QROWS))


def combine_kernel(parts_ref, self_ref, self_lse_ref, weight_ref, out_ref, attended_ref):
    @pl.when(pl.program_id(0) == 0)
    def _():
        blocks = parts_ref.shape[0] // 8
        width = HEADS * HEAD_DIM
        terms = parts_ref[:, width:].astype(F32)
        lse = terms + pltpu.roll(terms, EXTRA - HEADS, 1) + pltpu.roll(terms, EXTRA - 2 * HEADS, 1)
        lse = lse.reshape(blocks, 8, EXTRA)
        peak = jnp.maximum(jnp.max(lse, axis=0), self_lse_ref[...])
        scale = jnp.exp2(lse - peak[None])
        self_scale = jnp.exp2(self_lse_ref[...] - peak)
        inverse = 1.0 / (jnp.sum(scale, axis=0) + self_scale)
        scale = scale * inverse[None]
        self_scale = self_scale * inverse
        for head in range(HEADS):
            total = self_ref[:, head_cols(head)] * self_scale[:, head : head + 1]
            part = parts_ref[:, head_cols(head)].astype(F32).reshape(blocks, 8, HEAD_DIM)
            total = total + jnp.sum(part * scale[:, :, head : head + 1], axis=0)
            attended_ref[:, head_cols(head)] = total

    out_ref[0] = jnp.dot(
        attended_ref[...].astype(BF16), weight_ref[...], preferred_element_type=F32
    )


def combine_part(parts, self_out, self_lse, out_weight):
    depth, columns = out_weight.shape
    step = columns // 4
    whole = lambda i: (0, 0)
    return pl.pallas_call(
        combine_kernel,
        out_shape=jax.ShapeDtypeStruct((4, 8, step), F32),
        grid=(4,),
        in_specs=[
            pl.BlockSpec(parts.shape, whole),
            pl.BlockSpec(self_out.shape, whole),
            pl.BlockSpec(self_lse.shape, whole),
            pl.BlockSpec((depth, step), lambda i: (0, i)),
        ],
        out_specs=pl.BlockSpec((1, 8, step), lambda i: (i, 0, 0)),
        scratch_shapes=[pltpu.VMEM((8, depth), F32)],
        compiler_params=pltpu.CompilerParams(vmem_limit_bytes=VMEM_LIMIT),
        cost_estimate=pl.CostEstimate(flops=2 * 8 * depth * columns, bytes_accessed=9 << 20, transcendentals=0),
        name="question_merge",
    )(parts, self_out, self_lse, out_weight)


def local_kernel(query_ref, key_ref, value_ref, sum_ref, stat_ref):
    kv, tile = pl.program_id(0), pl.program_id(1)
    row_ids = lax.broadcasted_iota(jnp.int32, (TILE, TILE), 0)
    col_ids = lax.broadcasted_iota(jnp.int32, (TILE, TILE), 1)
    causal = col_ids <= row_ids
    for at in range(BLOCK // TILE):

        @pl.when(tile == at)
        def _(at=at):
            before = at * TILE
            for head in range(GROUP):
                queries = query_ref[:, head_cols(head)]
                scores = scores_of(queries, key_ref[: before + TILE, :])
                last = jnp.where(causal, scores[:, before:], -jnp.inf)
                if before:
                    scores = jnp.concatenate([scores[:, :before], last], axis=1)
                else:
                    scores = last
                maxima, weights, totals = weigh(scores)
                sum_ref[:, head_cols(head)] = times_values(weights, value_ref[: before + TILE, :])
                stat_ref[0, :, head : head + 1] = maxima
                stat_ref[0, :, GROUP + head : GROUP + head + 1] = totals


def local_part(ctx_query, ctx_key, ctx_value):
    rows, width = ctx_query.shape
    group = GROUP * HEAD_DIM
    return pl.pallas_call(
        local_kernel,
        out_shape=(
            jax.ShapeDtypeStruct((rows, width), F32),
            jax.ShapeDtypeStruct((2, rows, EXTRA), F32),
        ),
        grid=(2, rows // TILE),
        in_specs=[
            pl.BlockSpec((TILE, group), lambda kv, tile: (tile, kv)),
            pl.BlockSpec((rows, HEAD_DIM), lambda kv, tile: (0, kv)),
            pl.BlockSpec((rows, HEAD_DIM), lambda kv, tile: (0, kv)),
        ],
        out_specs=(
            pl.BlockSpec((TILE, group), lambda kv, tile: (tile, kv)),
            pl.BlockSpec((1, TILE, EXTRA), lambda kv, tile: (kv, tile, 0)),
        ),
        compiler_params=pltpu.CompilerParams(vmem_limit_bytes=VMEM_LIMIT),
        cost_estimate=pl.CostEstimate(
            flops=4 * rows * width * BLOCK, bytes_accessed=8 << 20, transcendentals=rows * HEADS * BLOCK // 2
        ),
        name="context_own",
    )(ctx_query, ctx_key, ctx_value)


def anchor_kernel(place_ref, query_ref, key_ref, value_ref, sum_ref, stat_ref, *rest):
    out_ref = rest[-1]
    is_anchor = place_ref[1] == 0
    for head in range(GROUP):
        scores = scores_of(query_ref[:, head_cols(head)], key_ref[...])
        maxima, weights, totals = weigh(scores)
        summed = times_values(weights, value_ref[...])
        own_max = stat_ref[0, :, head : head + 1]
        own_total = stat_ref[0, :, GROUP + head : GROUP + head + 1]
        maxima = jnp.where(is_anchor, -jnp.inf, maxima)
        peak = jnp.maximum(maxima, own_max)
        scale = jnp.exp2((maxima - peak) * SCALE)
        own_scale = jnp.exp2((own_max - peak) * SCALE)
        inverse = 1.0 / (totals * scale + own_total * own_scale)
        out_ref[:, head_cols(head)] = (
            summed * (scale * inverse) + sum_ref[:, head_cols(head)] * (own_scale * inverse)
        ).astype(BF16)


def anchor_part(place, ctx_query, keys, values, own_sum, own_stat, so_far):
    rows, width = ctx_query.shape
    group = GROUP * HEAD_DIM
    tile_of = lambda tile, place: (tile, place[0])
    whole = lambda tile, place: (0, 0)
    operands = [ctx_query, keys, values, own_sum, own_stat]
    in_specs = [
        pl.BlockSpec((TILE, group), tile_of),
        pl.BlockSpec((rows, HEAD_DIM), whole),
        pl.BlockSpec((rows, HEAD_DIM), whole),
        pl.BlockSpec((TILE, group), tile_of),
        pl.BlockSpec((1, TILE, EXTRA), lambda tile, place: (place[0], tile, 0)),
    ]
    aliases = {}
    if so_far is not None:
        operands.append(so_far)
        in_specs.append(pl.BlockSpec(memory_space=pl.ANY))
        aliases = {6: 0}
    return pl.pallas_call(
        anchor_kernel,
        out_shape=jax.ShapeDtypeStruct((rows, width), BF16),
        grid_spec=pltpu.PrefetchScalarGridSpec(
            num_scalar_prefetch=1,
            grid=(rows // TILE,),
            in_specs=in_specs,
            out_specs=pl.BlockSpec((TILE, group), tile_of),
        ),
        input_output_aliases=aliases,
        compiler_params=pltpu.CompilerParams(vmem_limit_bytes=VMEM_LIMIT),
        cost_estimate=pl.CostEstimate(
            flops=2 * rows * width * BLOCK, bytes_accessed=6 << 20, transcendentals=rows * GROUP * BLOCK
        ),
        name="context_anchor",
    )(place, *operands)


def device_at(z, y, core):
    return (z * 4 + y) * 2 + core


def edges(phase, steps):
    pairs = []
    for core in range(2):
        for first, last in steps:
            for other in range(1 if phase == 0 else 4):
                along_y = (core == 0) == (phase == 0)
                ends = [
                    device_at(other, at, core) if along_y else device_at(at, other, core)
                    for at in (first, last)
                ]
                pairs.append(tuple(ends))
    return pairs


SIBLINGS = [(at, at ^ 1) for at in range(32)]


def per_device(
    ctx_query, ctx_key, ctx_value, quest_query, quest_key, quest_value, quest_order, out_weight
):
    me = lax.axis_index("ctx")
    core = lax.rem(me, 2)
    first_half = jnp.concatenate([ctx_key[:, :HEAD_DIM], ctx_value[:, :HEAD_DIM]], axis=0)
    second_half = jnp.concatenate([ctx_key[:, HEAD_DIM:], ctx_value[:, HEAD_DIM:]], axis=0)
    moved = lax.ppermute(second_half, "ctx", [(0, 1)])
    half = jnp.where(me == 0, first_half, moved)
    for phase in range(2):
        half = half + lax.ppermute(half, "ctx", edges(phase, [(0, 1)]))
        half = half + lax.ppermute(half, "ctx", edges(phase, [(0, 3), (1, 2)]))
    other_half = lax.ppermute(half, "ctx", SIBLINGS)

    parts = question_part(quest_query, ctx_key, ctx_value)
    parts = lax.all_to_all(
        parts.reshape(32, 8, parts.shape[1]), "ctx", split_axis=0, concat_axis=0, tiled=True
    ).reshape(parts.shape)
    place = jnp.stack([me, me]).astype(jnp.int32)
    self_out, self_lse = self_part(place, quest_query, quest_key, quest_value, quest_order)
    own_sum, own_stat = local_part(ctx_query, ctx_key, ctx_value)
    projected = combine_part(parts, self_out, self_lse, out_weight)
    projected = lax.all_to_all(projected, "head", split_axis=0, concat_axis=0, tiled=True)
    answer = jnp.sum(projected, axis=0).astype(BF16)
    here = jnp.stack([core, me]).astype(jnp.int32)
    there = jnp.stack([1 - core, me]).astype(jnp.int32)
    ctx_out = anchor_part(here, ctx_query, half[:BLOCK], half[BLOCK:], own_sum, own_stat, None)
    ctx_out = anchor_part(
        there, ctx_query, other_half[:BLOCK], other_half[BLOCK:], own_sum, own_stat, ctx_out
    )
    return (ctx_out, answer)


def solution(mesh):
    in_specs = (
        P("ctx", "head"),
        P("ctx", "head"),
        P("ctx", "head"),
        P(None, "head"),
        P(None, "head"),
        P(None, "head"),
        P(),
        P("head", None),
    )
    out_specs = (P("ctx", "head"), P("ctx", "head"))
    return jax.shard_map(
        per_device, mesh=mesh, in_specs=in_specs, out_specs=out_specs, check_vma=False
    )
```

time: 309 us -> 116 us (0.38)
  blocking collectives: 134 us -> 0 us
  matrix products: 93.7 us -> 0 us
  Pallas kernels: 0 us -> 61 us
  starting transfers between devices: 0.12 us -> 24.9 us
  other arithmetic: 29.9 us -> 6 us
  local copies, waits for them, and re-layouts: 25.7 us -> 5.5 us
  between operations: 14.7 us -> 0.72 us
  waiting for transfers between devices: 8.01 us -> 16.6 us
    dot_general x9 -> x0, matrix products: 93.7 us -> none  [the longest x4 47.3 us: attend_block(): jnp.einsum('rkgd,ckd->kgrc', query_heads, key_heads, preferred_element_ty...]
    unnamed x1 -> x0, blocking collectives: 68.1 us -> none
    pmax x1 -> x0, blocking collectives: 66.2 us -> none  [per_device(): ctx_peak = lax.pmax(block_max, 'ctx')]
    pallas_call x0 -> x6, Pallas kernels: none -> 61 us  [the longest x2 32 us: anchor_part(): pl.pallas_call(anchor_kernel, out_shape=jax.ShapeDtypeStruct((rows, width...]
    reduce_sum x3 -> x1, other arithmetic: 19.6 us -> 0.62 us  [per_device(): answer = jnp.sum(projected, axis=0).astype(BF16)]
    ppermute x0 -> x6, waiting for transfers between devices: none -> 15 us  [the longest x2 6.08 us: per_device(): half = half + lax.ppermute(half, 'ctx', edges(phase, [(0, 1)]))]
    reshape x13 -> x0, local copies, waits for them, and re-layouts: 12.6 us -> none  [the longest x2 4.83 us: attend_block(): weighted.reshape(row_count, -1)]
    all_to_all x0 -> x2, starting transfers between devices: none -> 12.5 us  [the longest x1 8.13 us: per_device(): lax.all_to_all(parts.reshape(32, 8, parts.shape[1]), 'ctx', split_axis=0,...]
  transfers between devices with their start and end apart: 3 -> 8, of which waited for: 1 -> 4; matrix products, arithmetic and copies ran while one was open for 45% -> 6% of each run, Pallas kernels for 0% -> 39%
where the time goes in v1:
time: 116 us; the launch traced here: 115 us
  Pallas kernels  61 us (53%)
  starting transfers between devices  24.9 us (21%)
  waiting for transfers between devices  16.6 us (14%)
  other arithmetic  6 us (5%)
  local copies, waits for them, and re-layouts  5.5 us (5%)
    pallas_call x2, Pallas kernels, anchor_part(): pl.pallas_call(anchor_kernel, out_shape=jax.ShapeDtypeStruct((rows, width...  32 us
    pallas_call x1, Pallas kernels, local_part(): pl.pallas_call(local_kernel, out_shape=(jax.ShapeDtypeStruct((rows, width...  13.6 us
    all_to_all x1, starting transfers between devices, per_device(): lax.all_to_all(parts.reshape(32, 8, parts.shape[1]), 'ctx', split_axis=0,...  8.13 us
    ppermute x2, starting transfers between devices, per_device(): half = half + lax.ppermute(half, 'ctx', edges(phase, [(0, 3), (1, 2)]))  6.62 us
    ppermute x2, waiting for transfers between devices, per_device(): half = half + lax.ppermute(half, 'ctx', edges(phase, [(0, 1)]))  6.08 us
    ppermute x2, waiting for transfers between devices, per_device(): half = half + lax.ppermute(half, 'ctx', edges(phase, [(0, 3), (1, 2)]))  6.08 us
    pallas_call x1, Pallas kernels, combine_part(): pl.pallas_call(combine_kernel, out_shape=jax.ShapeDtypeStruct((4, 8, step...  6.02 us
    pallas_call x1, Pallas kernels, question_part(): pl.pallas_call(question_kernel, out_shape=jax.ShapeDtypeStruct((rows, wid...  5.1 us
  transfers between devices with their start and end apart: 8, of which 4 were waited for; matrix products, arithmetic and copies ran while one was open for 6% of the time, Pallas kernels for 39%

profile of v1, /device:TPU:1, one launch (start us, length us, event | category | flops | bytes accessed | tf_op | source)
XLA Modules:
  0.0 114.7 jit_solution(14342273646678015448)
XLA Ops:
  0.6 1.3 %fusion.2 = (bf16[1024,128]{1,0:T(8,128)(2,1)S(1)}, bf16[1024,128]{1,0:T(8,128)(2,1)S(1)}, bf16[1024,128]{1,0:T(8,128)(2,1)S(1)}, bf16[1024,128]{1,0:T(8,128)(2,1)S(1)}) fusion(bf16[1024,256]{1,0:T(8,128)(2,1)} %key_ref.4, bf16[1024,256]{1,0:T(8,128)(2,1)} %value_ref.4), kind=kLoop, calls=%fused_computation.7 | loop fusion | bytes 2097152 | tf_op jit(solution)/shard_map/slice | solution.py:299
  1.9 1.3 %collective-permute-start = (bf16[2048,128]{1,0:T(8,128)(2,1)S(1)}, bf16[2048,128]{1,0:T(8,128)(2,1)S(1)}, u32[]{:S(2)}, u32[]{:S(2)}) collective-permute-start(bf16[2048,128]{1,0:T(8,128)(2,1)S(1)} %pad_maximum_fusion), channel_id=1, source_target_pairs={{0,4},{1,5},{2,6},{3,7}} | collective-permute-start | bytes 1572872 | tf_op jit(solution)/shard_map/ppermute | solution.py:301
  3.3 2.8 %collective-permute-done = bf16[2048,128]{1,0:T(8,128)(2,1)S(1)} collective-permute-done((bf16[2048,128]{1,0:T(8,128)(2,1)S(1)}, bf16[2048,128]{1,0:T(8,128)(2,1)S(1)}, u32[]{:S(2)}, u32[]{:S(2)}) %collective-permute-start) | collective-permute-done | bytes 524320 | tf_op jit(solution)/shard_map/ppermute | solution.py:301
  6.1 0.1 maximum_select_fusion
  6.2 1.5 %collective-permute-start.1 = (bf16[2048,128]{1,0:T(8,128)(2,1)S(1)}, bf16[2048,128]{1,0:T(8,128)(2,1)S(1)}, u32[]{:S(2)}, u32[]{:S(2)}) collective-permute-start(bf16[2048,128]{1,0:T(8,128)(2,1)S(1)} %maximum_select_fusion), channel_id=1, source_target_pairs={{0,8},{4,36},{1,9},{5,37},{2,10},{6,38},{3,11},{7,39}} | collective-permute-start | bytes 1572872 | tf_op jit(solution)/shard_map/ppermute | solution.py:304
  7.7 6.1 %collective-permute-done.1 = bf16[2048,128]{1,0:T(8,128)(2,1)S(1)} collective-permute-done((bf16[2048,128]{1,0:T(8,128)(2,1)S(1)}, bf16[2048,128]{1,0:T(8,128)(2,1)S(1)}, u32[]{:S(2)}, u32[]{:S(2)}) %collective-permute-start.1) | collective-permute-done | bytes 524320 | tf_op jit(solution)/shard_map/ppermute | solution.py:304
  13.7 0.1 add.12
  13.9 1.3 %collective-permute-start.2 = (bf16[2048,128]{1,0:T(8,128)(2,1)S(1)}, bf16[2048,128]{1,0:T(8,128)(2,1)S(1)}, u32[]{:S(2)}, u32[]{:S(2)}) collective-permute-start(bf16[2048,128]{1,0:T(8,128)(2,1)S(1)} %add.12), channel_id=1, source_target_pairs={{0,24},{8,16},{4,100},{36,68},{1,25},{9,17},{5,101},{37,69},{2,26}... | collective-permute-start | bytes 1572872 | tf_op jit(solution)/shard_map/ppermute | solution.py:305
  15.2 6.1 %collective-permute-done.2 = bf16[2048,128]{1,0:T(8,128)(2,1)S(1)} collective-permute-done((bf16[2048,128]{1,0:T(8,128)(2,1)S(1)}, bf16[2048,128]{1,0:T(8,128)(2,1)S(1)}, u32[]{:S(2)}, u32[]{:S(2)}) %collective-permute-start.2) | collective-permute-done | bytes 524320 | tf_op jit(solution)/shard_map/ppermute | solution.py:305
  21.3 0.1 add.13
  21.4 2.1 %collective-permute-start.3 = (bf16[2048,128]{1,0:T(8,128)(2,1)S(1)}, bf16[2048,128]{1,0:T(8,128)(2,1)}, u32[]{:S(2)}, u32[]{:S(2)}) collective-permute-start(bf16[2048,128]{1,0:T(8,128)(2,1)S(1)} %add.13), channel_id=1, source_target_pairs={{0,32},{8,40},{16,48},{24,56},{4,12},{36,44},{68,76},{100,108},{1,... | collective-permute-start | bytes 1572872 | tf_op jit(solution)/shard_map/ppermute | solution.py:304
  23.5 5.1 %question_block.1 = bf16[256,1152]{1,0:T(8,128)(2,1)} custom-call(bf16[256,1024]{1,0:T(8,128)(2,1)S(1)} %copy-done.7, bf16[1024,256]{1,0:T(8,128)(2,1)S(1)} %copy-done.1, bf16[1024,256]{1,0:T(8,128)(2,1)S(1)} %copy-done.3), custom_call_target="tpu_custom_call" | custom-call | flops 1073741824 | bytes 2097152 | tf_op jit(solution)/shard_map/question_block/pallas_call | solution.py:60
  28.6 8.1 %all-to-all-start = ((bf16[32,8,1152]{2,1,0:T(8,128)(2,1)}), bf16[32,8,1152]{2,1,0:T(8,128)(2,1)}, u32[]{:S(2)}, u32[]{:S(2)}) async-start(bf16[32,8,1152]{2,1,0:T(8,128)(2,1)} %bitcast.3), calls=%async_computation | async-start | bytes 1179648 | tf_op jit(solution)/shard_map/all_to_all | solution.py:309
  36.8 0.6 pad_add_fusion.2.place_ref
  37.4 2.0 %add.14 = bf16[2048,128]{1,0:T(8,128)(2,1)} add(bf16[2048,128]{1,0:T(8,128)(2,1)S(1)} %add.13, bf16[2048,128]{1,0:T(8,128)(2,1)} %collective-permute-done.3) | non-fusion elementwise | flops 262144 | bytes 1572864 | tf_op jit(solution)/shard_map/add | solution.py:304
  39.4 5.3 %collective-permute-start.4 = (bf16[2048,128]{1,0:T(8,128)(2,1)}, bf16[2048,128]{1,0:T(8,128)(2,1)}, u32[]{:S(2)}, u32[]{:S(2)}) collective-permute-start(bf16[2048,128]{1,0:T(8,128)(2,1)} %add.14), channel_id=1, source_target_pairs={{0,96},{8,104},{16,112},{24,120},{32,64},{40,72},{48,80},{56,88},{... | collective-permute-start | bytes 1572872 | tf_op jit(solution)/shard_map/ppermute | solution.py:305
  44.7 4.3 %question_self.1 = (f32[8,1024]{1,0:T(8,128)}, f32[8,128]{1,0:T(8,128)}) custom-call(s32[2]{0:T(128)} %pad_add_fusion.2.place_ref, s32[256]{0:T(256)} %order_ref.1, bf16[256,1024]{1,0:T(8,128)(2,1)} %query_ref.9, bf16[256,256]{1,0:T(8,128)(2,1)} %key_ref.5, bf16[256,256]{1,0:T(8,128)(2,1)} %value_ref.5, s32[1,256]{1,0:T(1,128)} %bitcast.6), custom_call_target="tpu_custom_call" | custom-call | flops 268435456 | bytes 524288 | tf_op jit(solution)/shard_map/question_self/pallas_call | solution.py:98
  49.0 0.1 pad_add_fusion.1.place_ref
  49.1 1.0 copy-done.2
  50.1 1.0 copy-done.4
  51.1 13.6 %context_own.1 = (f32[1024,1024]{1,0:T(8,128)}, f32[2,1024,128]{2,1,0:T(8,128)S(1)}) custom-call(bf16[1024,1024]{1,0:T(8,128)(2,1)S(1)} %copy-done, bf16[1024,256]{1,0:T(8,128)(2,1)S(1)} %copy-done.2, bf16[1024,256]{1,0:T(8,128)(2,1)S(1)} %copy-done.4), custom_call_target="tpu_custom_call" | custom-call | flops 4294967296 | bytes 8388608 | tf_op jit(solution)/shard_map/context_own/pallas_call | solution.py:194
  64.8 6.0 %question_merge.1 = f32[4,8,1024]{2,1,0:T(8,128)} custom-call(bf16[256,1152]{1,0:T(8,128)(2,1)} %bitcast.4.parts_ref, f32[8,1024]{1,0:T(8,128)S(1)} %copy-done.5, f32[8,128]{1,0:T(8,128)S(1)} %copy-done.6, bf16[1024,4096]{1,0:T(8,128)(2,1)} %weight_ref.1), custom_call_target="tpu_custom_call" | custom-call | flops 67108864 | bytes 9437184 | tf_op jit(solution)/shard_map/question_merge/pallas_call | solution.py:149
  70.8 4.3 %all-to-all-start.1 = ((f32[4,8,1024]{2,1,0:T(8,128)}), f32[4,8,1024]{2,1,0:T(8,128)S(1)}, u32[]{:S(2)}, u32[]{:S(2)}) async-start(f32[4,8,1024]{2,1,0:T(8,128)} %question_merge.1), calls=%async_computation.1 | async-start | bytes 262144 | tf_op jit(solution)/shard_map/all_to_all | solution.py:316
  75.1 2.1 %add.15 = bf16[2048,128]{1,0:T(8,128)(2,1)} add(bf16[2048,128]{1,0:T(8,128)(2,1)} %add.14, bf16[2048,128]{1,0:T(8,128)(2,1)} %collective-permute-done.4) | non-fusion elementwise | flops 262144 | bytes 1572864 | tf_op jit(solution)/shard_map/add | solution.py:305
  77.3 1.0 collective-permute-start.5
  78.2 0.1 pad_add_fusion.place_ref
  78.3 1.6 %all-to-all-done.1 = f32[4,8,1024]{2,1,0:T(8,128)S(1)} async-done(((f32[4,8,1024]{2,1,0:T(8,128)}), f32[4,8,1024]{2,1,0:T(8,128)S(1)}, u32[]{:S(2)}, u32[]{:S(2)}) %all-to-all-start.1) | async-done | bytes 131104 | tf_op jit(solution)/shard_map/all_to_all | solution.py:316
  80.0 0.6 reduce_sum.9
  80.6 1.1 fusion
  81.6 16.0 %context_anchor.2.rest_0_ = bf16[1024,1024]{1,0:T(8,128)(2,1)} custom-call(s32[2]{0:T(128)S(1)} %pad_add_fusion.1.place_ref, bf16[1024,1024]{1,0:T(8,128)(2,1)S(1)} %copy-done, bf16[1024,128]{1,0:T(8,128)(2,1)S(1)} %get-tuple-element.11.key_ref, bf16[1024,128]{1,0:T(8,128)(2,1)S(1)} %get-tuple-element.10.value_ref, f32[1024,1024]{1,0:T(8,128)} %get-tuple-element.6.sum_ref, ...), custom_call_target="tpu_custom_call" | custom-call | flops 2147483648 | bytes 6291456 | tf_op jit(solution)/shard_map/context_anchor/pallas_call | solution.py:255
  97.6 1.1 fusion.1
  98.7 16.0 %context_anchor.3 = bf16[1024,1024]{1,0:T(8,128)(2,1)} custom-call(s32[2]{0:T(128)S(1)} %pad_add_fusion.place_ref, bf16[1024,1024]{1,0:T(8,128)(2,1)S(1)} %copy-done, bf16[1024,128]{1,0:T(8,128)(2,1)S(1)} %get-tuple-element.13.key_ref, bf16[1024,128]{1,0:T(8,128)(2,1)S(1)} %get-tuple-element.12.value_ref, ...), custom_call_target="tpu_custom_call", output_to_operand_aliasing={{}: (6, {})} | custom-call | flops 2147483648 | bytes 6291456 | tf_op jit(solution)/shard_map/context_anchor/pallas_call | solution.py:255
  (19 shorter events, 0.1 us)
Async XLA Ops:
  1.9 4.1 %collective-permute-start = (bf16[2048,128]{1,0:T(8,128)(2,1)S(1)}, bf16[2048,128]{1,0:T(8,128)(2,1)S(1)}, u32[]{:S(2)}, u32[]{:S(2)}) collective-permute-start(bf16[2048,128]{1,0:T(8,128)(2,1)S(1)} %pad_maximum_fusion), channel_id=1, source_target_pairs={{0,4},{1,5},{2,6},{3,7}} | collective-permute-start | bytes 1572872 | tf_op jit(solution)/shard_map/ppermute | solution.py:301
  6.0 17.5 %copy-start.1 = (bf16[1024,256]{1,0:T(8,128)(2,1)S(1)}, bf16[1024,256]{1,0:T(8,128)(2,1)}, u32[]{:S(2)}) copy-start(bf16[1024,256]{1,0:T(8,128)(2,1)} %key_ref.4) | copy-start | bytes 1572868
  6.1 17.5 %copy-start.3 = (bf16[1024,256]{1,0:T(8,128)(2,1)S(1)}, bf16[1024,256]{1,0:T(8,128)(2,1)}, u32[]{:S(2)}) copy-start(bf16[1024,256]{1,0:T(8,128)(2,1)} %value_ref.4) | copy-start | bytes 1572868
  6.1 17.5 %copy-start.7 = (bf16[256,1024]{1,0:T(8,128)(2,1)S(1)}, bf16[256,1024]{1,0:T(8,128)(2,1)}, u32[]{:S(2)}) copy-start(bf16[256,1024]{1,0:T(8,128)(2,1)} %query_ref.9) | copy-start | bytes 1572868
  6.2 7.5 %collective-permute-start.1 = (bf16[2048,128]{1,0:T(8,128)(2,1)S(1)}, bf16[2048,128]{1,0:T(8,128)(2,1)S(1)}, u32[]{:S(2)}, u32[]{:S(2)}) collective-permute-start(bf16[2048,128]{1,0:T(8,128)(2,1)S(1)} %maximum_select_fusion), channel_id=1, source_target_pairs={{0,8},{4,36},{1,9},{5,37},{2,10},{6,38},{3,11},{7,39}} | collective-permute-start | bytes 1572872 | tf_op jit(solution)/shard_map/ppermute | solution.py:304
  13.9 7.4 %collective-permute-start.2 = (bf16[2048,128]{1,0:T(8,128)(2,1)S(1)}, bf16[2048,128]{1,0:T(8,128)(2,1)S(1)}, u32[]{:S(2)}, u32[]{:S(2)}) collective-permute-start(bf16[2048,128]{1,0:T(8,128)(2,1)S(1)} %add.12), channel_id=1, source_target_pairs={{0,24},{8,16},{4,100},{36,68},{1,25},{9,17},{5,101},{37,69},{2,26}... | collective-permute-start | bytes 1572872 | tf_op jit(solution)/shard_map/ppermute | solution.py:305
  21.4 16.0 %collective-permute-start.3 = (bf16[2048,128]{1,0:T(8,128)(2,1)S(1)}, bf16[2048,128]{1,0:T(8,128)(2,1)}, u32[]{:S(2)}, u32[]{:S(2)}) collective-permute-start(bf16[2048,128]{1,0:T(8,128)(2,1)S(1)} %add.13), channel_id=1, source_target_pairs={{0,32},{8,40},{16,48},{24,56},{4,12},{36,44},{68,76},{100,108},{1,... | collective-permute-start | bytes 1572872 | tf_op jit(solution)/shard_map/ppermute | solution.py:304
  28.6 20.4 %copy-start = (bf16[1024,1024]{1,0:T(8,128)(2,1)S(1)}, bf16[1024,1024]{1,0:T(8,128)(2,1)}, u32[]{:S(2)}) copy-start(bf16[1024,1024]{1,0:T(8,128)(2,1)} %query_ref.7) | copy-start | bytes 6291460
  28.6 36.1 %all-to-all-start = ((bf16[32,8,1152]{2,1,0:T(8,128)(2,1)}), bf16[32,8,1152]{2,1,0:T(8,128)(2,1)}, u32[]{:S(2)}, u32[]{:S(2)}) async-start(bf16[32,8,1152]{2,1,0:T(8,128)(2,1)} %bitcast.3), calls=%async_computation | async-start | bytes 1179648 | tf_op jit(solution)/shard_map/all_to_all | solution.py:309
  39.4 35.7 %collective-permute-start.4 = (bf16[2048,128]{1,0:T(8,128)(2,1)}, bf16[2048,128]{1,0:T(8,128)(2,1)}, u32[]{:S(2)}, u32[]{:S(2)}) collective-permute-start(bf16[2048,128]{1,0:T(8,128)(2,1)} %add.14), channel_id=1, source_target_pairs={{0,96},{8,104},{16,112},{24,120},{32,64},{40,72},{48,80},{56,88},{... | collective-permute-start | bytes 1572872 | tf_op jit(solution)/shard_map/ppermute | solution.py:305
  49.1 1.0 copy-start.2
  50.1 1.0 copy-start.4
  51.1 13.6 %copy-start.5 = (f32[8,1024]{1,0:T(8,128)S(1)}, f32[8,1024]{1,0:T(8,128)}, u32[]{:S(2)}) copy-start(f32[8,1024]{1,0:T(8,128)} %get-tuple-element.8.self_ref) | copy-start | bytes 98308
  51.1 13.6 %copy-start.6 = (f32[8,128]{1,0:T(8,128)S(1)}, f32[8,128]{1,0:T(8,128)}, u32[]{:S(2)}) copy-start(f32[8,128]{1,0:T(8,128)} %get-tuple-element.9.self_lse_ref) | copy-start | bytes 12292
  70.8 9.2 %all-to-all-start.1 = ((f32[4,8,1024]{2,1,0:T(8,128)}), f32[4,8,1024]{2,1,0:T(8,128)S(1)}, u32[]{:S(2)}, u32[]{:S(2)}) async-start(f32[4,8,1024]{2,1,0:T(8,128)} %question_merge.1), calls=%async_computation.1 | async-start | bytes 262144 | tf_op jit(solution)/shard_map/all_to_all | solution.py:316
  77.3 20.4 %collective-permute-start.5 = (bf16[2048,128]{1,0:T(8,128)(2,1)}, bf16[2048,128]{1,0:T(8,128)(2,1)}, u32[]{:S(2)}, u32[]{:S(2)}) collective-permute-start(bf16[2048,128]{1,0:T(8,128)(2,1)} %add.15), channel_id=1, source_target_pairs={{0,4},{4,0},{8,12},{12,8},{16,20},{20,16},{24,28},{28,24},{32,36},... | collective-permute-start | bytes 1572872 | tf_op jit(solution)/shard_map/ppermute | solution.py:306

commit v2 on v0

v2 whole, which is shorter than its diff:
```python
import math

import jax
import jax.numpy as jnp
from jax import lax
from jax.experimental import pallas as pl
from jax.experimental.pallas import tpu as pltpu
from jax.sharding import PartitionSpec as P

HEAD_DIM = 128
BLOCK = 1024
TILE = 256
QROWS = 256
GROUP = 4
HEADS = 8
EXTRA = 128
SCALE = math.log2(math.e) / math.sqrt(HEAD_DIM)
F32 = jnp.float32
BF16 = jnp.bfloat16
VMEM_LIMIT = 56 * 1024 * 1024
ANCHOR_ROWS = 512


def scores_of(queries, keys):
    return lax.dot_general(queries, keys, (((1,), (1,)), ((), ())), preferred_element_type=F32)


def weigh(scores):
    maxima = jnp.max(scores, axis=-1, keepdims=True)
    weights = jnp.exp2((scores - maxima) * SCALE)
    return maxima, weights, jnp.sum(weights, axis=-1, keepdims=True)


def whole(*shape):
    return pl.BlockSpec(shape, lambda step: (0,) * len(shape))


def columns_of(rows, width, at):
    return pl.BlockSpec((rows, width), lambda step: (0, at))


SCALARS = pl.BlockSpec(memory_space=pltpu.SMEM)
IN_HBM = pl.BlockSpec(memory_space=pltpu.HBM)


def times_values(weights, values):
    return jnp.dot(weights.astype(BF16), values, preferred_element_type=F32)


def head_cols(head):
    return slice(head * HEAD_DIM, (head + 1) * HEAD_DIM)


def staggered(items, scores_at, finish):
    scores = scores_at(items[0])
    for at, item in enumerate(items):
        later = scores_at(items[at + 1]) if at + 1 < len(items) else None
        finish(item, scores)
        scores = later


class Local:
    SCRATCH = [
        pltpu.VMEM((BLOCK, GROUP * HEAD_DIM), BF16),
        pltpu.VMEM((BLOCK, HEAD_DIM), BF16),
        pltpu.VMEM((BLOCK, HEAD_DIM), BF16),
        pltpu.VMEM((BLOCK, GROUP * HEAD_DIM), F32),
        pltpu.VMEM((BLOCK, EXTRA), F32),
        pltpu.SemaphoreType.DMA((BLOCK // TILE,)),
        pltpu.SemaphoreType.DMA((2 * (BLOCK // TILE),)),
        pltpu.SemaphoreType.DMA((2 * (BLOCK // TILE),)),
    ]

    def __init__(self, kv, hbm, scratch):
        self.query_hbm, self.key_hbm, self.value_hbm, self.sum_out, self.stat_out = hbm
        self.query_ref, self.key_ref, self.value_ref, self.sum_ref, self.stat_ref = scratch[:5]
        query_sems, kv_sems, self.sems = scratch[5:]
        query_cols = pl.ds(pl.multiple_of(kv * GROUP * HEAD_DIM, HEAD_DIM), GROUP * HEAD_DIM)
        kv_cols = pl.ds(pl.multiple_of(kv * HEAD_DIM, HEAD_DIM), HEAD_DIM)
        self.loads = []
        for tile in range(BLOCK // TILE):
            rows = pl.ds(tile * TILE, TILE)
            self.loads.append(
                [
                    pltpu.make_async_copy(
                        self.key_hbm.at[rows, kv_cols], self.key_ref.at[rows], kv_sems.at[2 * tile]
                    ),
                    pltpu.make_async_copy(
                        self.query_hbm.at[rows, query_cols], self.query_ref.at[rows], query_sems.at[tile]
                    ),
                    pltpu.make_async_copy(
                        self.value_hbm.at[rows, kv_cols], self.value_ref.at[rows], kv_sems.at[2 * tile + 1]
                    ),
                ]
            )

    def load(self):
        for tile in self.loads:
            for copy in tile:
                copy.start()

    def run(self):
        row_ids = lax.broadcasted_iota(jnp.int32, (TILE, TILE), 0)
        col_ids = lax.broadcasted_iota(jnp.int32, (TILE, TILE), 1)
        causal = col_ids <= row_ids
        lane = lax.broadcasted_iota(jnp.int32, (TILE, EXTRA), 1)
        stats, copies = {}, []

        def send(source, target, rows):
            copy = pltpu.make_async_copy(source.at[rows], target.at[rows], self.sems.at[len(copies)])
            copy.start()
            copies.append(copy)

        def scores_at(item):
            tile, head = item
            if head == 0:
                for copy in self.loads[tile]:
                    copy.wait()
            rows = slice(tile * TILE, (tile + 1) * TILE)
            return scores_of(self.query_ref[rows, head_cols(head)], self.key_ref[: (tile + 1) * TILE, :])

        def finish(item, scores):
            tile, head = item
            rows = slice(tile * TILE, (tile + 1) * TILE)
            before = tile * TILE
            last = jnp.where(causal, scores[:, before:], -jnp.inf)
            scores = jnp.concatenate([scores[:, :before], last], axis=1) if before else last
            maxima, weights, totals = weigh(scores)
            values = self.value_ref[: before + TILE, :]
            self.sum_ref[rows, head_cols(head)] = times_values(weights, values)
            stat = stats.get(tile, jnp.zeros((TILE, EXTRA), F32))
            stat = jnp.where(lane == head, maxima, stat)
            stats[tile] = jnp.where(lane == GROUP + head, totals, stat)
            if head == GROUP - 1:
                self.stat_ref[rows, :] = stats[tile]
                send(self.sum_ref, self.sum_out, rows)
                send(self.stat_ref, self.stat_out, rows)

        tiles = range(BLOCK // TILE)
        staggered([(tile, head) for tile in tiles for head in range(GROUP)], scores_at, finish)
        for copy in copies:
            copy.wait()


def local_kernel(place_ref, *refs):
    local = Local(place_ref[0], refs[:5], refs[5:])
    local.load()
    local.run()


LOCAL_OUT = (
    jax.ShapeDtypeStruct((BLOCK, GROUP * HEAD_DIM), F32),
    jax.ShapeDtypeStruct((BLOCK, EXTRA), F32),
)


def local_part(place, ctx_query, ctx_key, ctx_value):
    return pl.pallas_call(
        local_kernel,
        out_shape=LOCAL_OUT,
        grid=(1,),
        in_specs=[SCALARS] + [IN_HBM] * 3,
        out_specs=(IN_HBM,) * 2,
        scratch_shapes=Local.SCRATCH,
        compiler_params=pltpu.CompilerParams(vmem_limit_bytes=VMEM_LIMIT),
        cost_estimate=pl.CostEstimate(flops=1 << 26, bytes_accessed=1 << 18, transcendentals=1 << 16),
        name="context_own",
    )(place, ctx_query, ctx_key, ctx_value)


def question_kernel(
    place_ref,
    order_ref,
    query_ref,
    key_ref,
    value_ref,
    self_key_ref,
    self_value_ref,
    order_row_ref,
    ctx_query_hbm,
    ctx_key_hbm,
    ctx_value_hbm,
    out_ref,
    self_ref,
    self_lse_ref,
    sum_out,
    stat_out,
    *scratch,
):
    own = Local(
        place_ref[0] % 2, (ctx_query_hbm, ctx_key_hbm, ctx_value_hbm, sum_out, stat_out), scratch
    )
    own.load()
    lane = lax.broadcasted_iota(jnp.int32, (QROWS, EXTRA), 1)
    packed = [jnp.zeros((QROWS, EXTRA), F32)]
    first = pl.multiple_of((place_ref[0] // 2) * 16, 16)
    upper = place_ref[0] % 2 == 1
    row_ids = lax.broadcasted_iota(jnp.int32, (16, QROWS), 0)
    row_order = jnp.zeros((16, QROWS), jnp.int32)
    for row in range(16):
        row_order = jnp.where(row_ids == row, order_ref[first + row], row_order)
    allowed = jnp.concatenate([order_row_ref[...] <= row_order] * GROUP, axis=0)
    lse = jnp.zeros((8, EXTRA), F32)

    def scores_at(head):
        return scores_of(query_ref[:, head_cols(head)], key_ref[:, head_cols(head // GROUP)])

    def finish(head, scores):
        maxima, weights, totals = weigh(scores)
        summed = times_values(weights, value_ref[:, head_cols(head // GROUP)])
        out_ref[:, head_cols(head)] = (summed / totals).astype(BF16)
        packed[0] = jnp.where(lane == head, maxima * SCALE + jnp.log2(totals), packed[0])

    staggered(range(HEADS), scores_at, finish)
    rest, terms = packed[0], None
    for part in range(3):
        term = rest.astype(BF16).astype(F32)
        rest = rest - term
        terms = term if part == 0 else terms + pltpu.roll(term, part * HEADS, 1)
    out_ref[:, HEADS * HEAD_DIM :] = terms.astype(BF16)

    for kv in range(HEADS // GROUP):
        heads = range(kv * GROUP, (kv + 1) * GROUP)
        queries = jnp.concatenate(
            [query_ref[pl.ds(first, 16), head_cols(head)] for head in heads], axis=0
        )
        scores = scores_of(queries, self_key_ref[:, head_cols(kv)])
        maxima, weights, totals = weigh(jnp.where(allowed, scores, -jnp.inf))
        summed = times_values(weights, self_value_ref[:, head_cols(kv)]) / totals
        row_lse = maxima * SCALE + jnp.log2(totals)
        for at, head in enumerate(heads):
            low, high = slice(at * 16, at * 16 + 8), slice(at * 16 + 8, at * 16 + 16)
            self_ref[:, head_cols(head)] = jnp.where(upper, summed[high], summed[low])
            lse = jnp.where(lane[:8] == head, jnp.where(upper, row_lse[high], row_lse[low]), lse)
    self_lse_ref[...] = lse
    own.run()


def question_part(
    place, quest_query, ctx_query, ctx_key, ctx_value, quest_key, quest_value, quest_order
):
    rows, width = quest_query.shape
    return pl.pallas_call(
        question_kernel,
        out_shape=(
            jax.ShapeDtypeStruct((rows, width + EXTRA), BF16),
            jax.ShapeDtypeStruct((8, width), F32),
            jax.ShapeDtypeStruct((8, EXTRA), F32),
            *LOCAL_OUT,
        ),
        grid=(1,),
        in_specs=[
            SCALARS,
            SCALARS,
            whole(rows, width),
            whole(*ctx_key.shape),
            whole(*ctx_value.shape),
            whole(*quest_key.shape),
            whole(*quest_value.shape),
            whole(1, QROWS),
            IN_HBM,
            IN_HBM,
            IN_HBM,
        ],
        out_specs=(
            whole(rows, width + EXTRA),
            whole(8, width),
            whole(8, EXTRA),
            IN_HBM,
            IN_HBM,
        ),
        scratch_shapes=Local.SCRATCH,
        compiler_params=pltpu.CompilerParams(vmem_limit_bytes=VMEM_LIMIT),
        cost_estimate=pl.CostEstimate(flops=1 << 26, bytes_accessed=1 << 18, transcendentals=1 << 16),
        name="question_block",
    )(
        place,
        quest_order,
        quest_query,
        ctx_key,
        ctx_value,
        quest_key,
        quest_value,
        quest_order.reshape(1, QROWS),
        ctx_query,
        ctx_key,
        ctx_value,
    )


def combine_kernel(
    parts_hbm, self_ref, self_lse_ref, weight_hbm, out_ref, parts_ref, weight_ref, sems
):
    step = out_ref.shape[2]
    arrived = pltpu.make_async_copy(parts_hbm, parts_ref, sems.at[4])
    arrived.start()
    loads = []
    for at in range(out_ref.shape[0]):
        cols = pl.ds(at * step, step)
        loads.append(
            pltpu.make_async_copy(weight_hbm.at[:, cols], weight_ref.at[:, cols], sems.at[at])
        )
        loads[-1].start()
    arrived.wait()
    blocks = parts_ref.shape[0] // 8
    width = HEADS * HEAD_DIM
    terms = parts_ref[:, width:].astype(F32)
    lse = terms + pltpu.roll(terms, EXTRA - HEADS, 1) + pltpu.roll(terms, EXTRA - 2 * HEADS, 1)
    lse = lse.reshape(blocks, 8, EXTRA)
    peak = jnp.maximum(jnp.max(lse, axis=0), self_lse_ref[...])
    scale = jnp.exp2(lse - peak[None])
    self_scale = jnp.exp2(self_lse_ref[...] - peak)
    inverse = 1.0 / (jnp.sum(scale, axis=0) + self_scale)
    scale = scale * inverse[None]
    self_scale = self_scale * inverse
    attended = []
    for head in range(HEADS):
        total = self_ref[:, head_cols(head)] * self_scale[:, head : head + 1]
        part = parts_ref[:, head_cols(head)].astype(F32).reshape(blocks, 8, HEAD_DIM)
        attended.append(total + jnp.sum(part * scale[:, :, head : head + 1], axis=0))
    attended = jnp.concatenate(attended, axis=1).astype(BF16)
    for at, load in enumerate(loads):
        load.wait()
        out_ref[at] = jnp.dot(
            attended, weight_ref[:, at * step : (at + 1) * step], preferred_element_type=F32
        )


def combine_part(parts, self_out, self_lse, out_weight):
    depth, columns = out_weight.shape
    return pl.pallas_call(
        combine_kernel,
        out_shape=jax.ShapeDtypeStruct((4, 8, columns // 4), F32),
        grid=(1,),
        in_specs=[
            IN_HBM,
            whole(*self_out.shape),
            whole(*self_lse.shape),
            IN_HBM,
        ],
        out_specs=whole(4, 8, columns // 4),
        scratch_shapes=[
            pltpu.VMEM(parts.shape, BF16),
            pltpu.VMEM((depth, columns), BF16),
            pltpu.SemaphoreType.DMA((5,)),
        ],
        compiler_params=pltpu.CompilerParams(vmem_limit_bytes=VMEM_LIMIT),
        cost_estimate=pl.CostEstimate(flops=2 * 8 * depth * columns, bytes_accessed=9 << 20, transcendentals=0),
        name="question_merge",
    )(parts, self_out, self_lse, out_weight)


def anchor_kernel(place_ref, query_ref, key_ref, value_ref, sum_ref, stat_ref, *rest):
    out_ref, summed_ref = rest[-2:]
    is_anchor = place_ref[1] == 0
    lane = lax.broadcasted_iota(jnp.int32, (TILE, EXTRA), 1)
    packed = {}

    def scores_at(item):
        row, head = item
        return scores_of(query_ref[row : row + TILE, head_cols(head)], key_ref[...])

    def finish(item, scores):
        row, head = item
        rows = slice(row, row + TILE)
        maxima, weights, totals = weigh(scores)
        summed_ref[rows, head_cols(head)] = times_values(weights, value_ref[...])
        all_maxima, all_totals = packed.get(row, (jnp.zeros((TILE, EXTRA), F32),) * 2)
        all_maxima = jnp.where(lane == head, maxima, all_maxima)
        all_totals = jnp.where(lane == head, totals, all_totals)
        packed[row] = all_maxima, all_totals
        if head == GROUP - 1:
            merge(rows, all_maxima, all_totals)

    def merge(rows, maxima, totals):
        own_max = stat_ref[rows, :]
        own_total = pltpu.roll(own_max, EXTRA - GROUP, 1)
        maxima = jnp.where(is_anchor, -jnp.inf, maxima)
        peak = jnp.maximum(maxima, own_max)
        scale = jnp.exp2((maxima - peak) * SCALE)
        own_scale = jnp.exp2((own_max - peak) * SCALE)
        inverse = 1.0 / (totals * scale + own_total * own_scale)
        scale, own_scale = scale * inverse, own_scale * inverse
        for head in range(GROUP):
            cols = head_cols(head)
            out_ref[rows, cols] = (
                summed_ref[rows, cols] * scale[:, head : head + 1]
                + sum_ref[rows, cols] * own_scale[:, head : head + 1]
            ).astype(BF16)

    rows = range(0, ANCHOR_ROWS, TILE)
    staggered([(row, head) for row in rows for head in range(GROUP)], scores_at, finish)


def anchor_part(place, ctx_query, half, own_sum, own_stat, so_far):
    rows, width = ctx_query.shape
    group = GROUP * HEAD_DIM
    tile_of = lambda tile, place: (tile, place[0])
    row_of = lambda tile, place: (tile, 0)
    operands = [ctx_query, half, half, own_sum, own_stat]
    in_specs = [
        pl.BlockSpec((ANCHOR_ROWS, group), tile_of),
        pl.BlockSpec((BLOCK, HEAD_DIM), lambda tile, place: (0, 0)),
        pl.BlockSpec((BLOCK, HEAD_DIM), lambda tile, place: (0, 1)),
        pl.BlockSpec((ANCHOR_ROWS, group), row_of),
        pl.BlockSpec((ANCHOR_ROWS, EXTRA), row_of),
    ]
    aliases = {}
    if so_far is not None:
        operands.append(so_far)
        in_specs.append(pl.BlockSpec(memory_space=pl.ANY))
        aliases = {6: 0}
    return pl.pallas_call(
        anchor_kernel,
        out_shape=jax.ShapeDtypeStruct((rows, width), BF16),
        grid_spec=pltpu.PrefetchScalarGridSpec(
            num_scalar_prefetch=1,
            grid=(rows // ANCHOR_ROWS,),
            in_specs=in_specs,
            out_specs=pl.BlockSpec((ANCHOR_ROWS, group), tile_of),
            scratch_shapes=[pltpu.VMEM((ANCHOR_ROWS, group), F32)],
        ),
        input_output_aliases=aliases,
        compiler_params=pltpu.CompilerParams(vmem_limit_bytes=VMEM_LIMIT),
        cost_estimate=pl.CostEstimate(
            flops=1 << 26, bytes_accessed=1 << 18, transcendentals=1 << 16
        ),
        name="context_anchor",
    )(place, *operands)


def after(value, *others):
    return lax.optimization_barrier((value, *others))[0]


def exchange(value, axis, groups=None):
    return lax.all_to_all(
        value, axis, split_axis=0, concat_axis=0, axis_index_groups=groups, tiled=True
    )


def per_device(
    ctx_query, ctx_key, ctx_value, quest_query, quest_key, quest_value, quest_order, out_weight
):
    me = lax.axis_index("ctx").astype(jnp.int32)
    devices = lax.axis_size("ctx")
    core = lax.rem(me, 2)
    place = me.reshape(1)
    here, there = jnp.stack([core, me]), jnp.stack([1 - core, me])
    groups = [list(range(at, devices, 2)) for at in range(2)]
    siblings = [(at, at ^ 1) for at in range(devices)]
    first, second = slice(0, HEAD_DIM), slice(HEAD_DIM, 2 * HEAD_DIM)

    keys = lax.ppermute(ctx_key, "ctx", [(0, 1)])
    values = lax.ppermute(ctx_value, "ctx", [(0, 1)])
    half = jnp.where(
        me == 0,
        jnp.concatenate([ctx_key[:, first], ctx_value[:, first]], axis=1),
        jnp.concatenate([keys[:, second], values[:, second]], axis=1),
    )
    chips = devices // 2
    shares = exchange(half.reshape(chips, BLOCK // chips, 2 * HEAD_DIM), "ctx", groups)[0]

    parts, self_out, self_lse, *own_here = question_part(
        place, quest_query, ctx_query, ctx_key, ctx_value, quest_key, quest_value, quest_order
    )
    shares = after(shares, self_lse)
    half = exchange(jnp.broadcast_to(shares[None], (chips, *shares.shape)), "ctx", groups)
    own_there = local_part(after(there, shares), ctx_query, ctx_key, ctx_value)
    half = after(half.reshape(BLOCK, 2 * HEAD_DIM), own_there[1])
    other_half = lax.ppermute(half, "ctx", siblings)

    width = parts.shape[1]
    parts = exchange(after(parts, half).reshape(devices, -1, width), "ctx").reshape(QROWS, width)
    ctx_out = anchor_part(here, ctx_query, half, *own_here, None)
    parts = after(parts, ctx_out)
    projected = combine_part(parts, self_out, self_lse, out_weight)
    there = after(there, projected)
    projected = exchange(projected, "head")
    ctx_out = anchor_part(there, ctx_query, other_half, *own_there, ctx_out)
    answer = jnp.sum(after(projected, ctx_out), axis=0).astype(BF16)
    return (ctx_out, answer)


def solution(mesh):
    in_specs = (
        P("ctx", "head"),
        P("ctx", "head"),
        P("ctx", "head"),
        P(None, "head"),
        P(None, "head"),
        P(None, "head"),
        P(),
        P("head", None),
    )
    out_specs = (P("ctx", "head"), P("ctx", "head"))
    return jax.shard_map(
        per_device, mesh=mesh, in_specs=in_specs, out_specs=out_specs, check_vma=False
    )
```

time: 309 us -> 83.8 us (0.27)
  blocking collectives: 134 us -> 0 us
  matrix products: 93.7 us -> 0 us
  Pallas kernels: 0 us -> 43.8 us
  other arithmetic: 29.9 us -> 2.83 us
  starting transfers between devices: 0.12 us -> 26.1 us
  local copies, waits for them, and re-layouts: 25.7 us -> 4.46 us
  between operations: 14.7 us -> 0.76 us
    dot_general x9 -> x0, matrix products: 93.7 us -> none  [the longest x4 47.3 us: attend_block(): jnp.einsum('rkgd,ckd->kgrc', query_heads, key_heads, preferred_element_ty...]
    unnamed x1 -> x0, blocking collectives: 68.1 us -> none
    pmax x1 -> x0, blocking collectives: 66.2 us -> none  [per_device(): ctx_peak = lax.pmax(block_max, 'ctx')]
    pallas_call x0 -> x5, Pallas kernels: none -> 43.8 us  [the longest x2 19.9 us: anchor_part(): pl.pallas_call(anchor_kernel, out_shape=jax.ShapeDtypeStruct((rows, width...]
    all_to_all x0 -> x4, starting transfers between devices: none -> 23.2 us  [exchange(): lax.all_to_all(value, axis, split_axis=0, concat_axis=0, axis_index_group...]
    reduce_sum x3 -> x1, other arithmetic: 19.6 us -> 0.62 us  [per_device(): answer = jnp.sum(after(projected, ctx_out), axis=0).astype(BF16)]
    reshape x13 -> x0, local copies, waits for them, and re-layouts: 12.6 us -> none  [the longest x2 4.83 us: attend_block(): weighted.reshape(row_count, -1)]
    reduce_scatter x1 -> x0, waiting for transfers between devices: 7.96 us -> none  [per_device(): lax.psum_scatter(projected, 'head', scatter_dimension=1, tiled=True)]
  transfers between devices with their start and end apart: 3 -> 7, of which waited for: 1 -> 3; matrix products, arithmetic and copies ran while one was open for 45% -> 4% of each run, Pallas kernels for 0% -> 53%
where the time goes in v2:
time: 83.8 us; the launch traced here: 83 us
  Pallas kernels  43.8 us (52%)
  starting transfers between devices  26.1 us (31%)
  waiting for transfers between devices  4.99 us (6%)
  local copies, waits for them, and re-layouts  4.46 us (5%)
  other arithmetic  2.83 us (3%)
    all_to_all x4, starting transfers between devices, exchange(): lax.all_to_all(value, axis, split_axis=0, concat_axis=0, axis_index_group...  23.2 us
    pallas_call x2, Pallas kernels, anchor_part(): pl.pallas_call(anchor_kernel, out_shape=jax.ShapeDtypeStruct((rows, width...  19.9 us
    pallas_call x1, Pallas kernels, question_part(): pl.pallas_call(question_kernel, out_shape=(jax.ShapeDtypeStruct((rows, wi...  11.5 us
    pallas_call x1, Pallas kernels, local_part(): pl.pallas_call(local_kernel, out_shape=LOCAL_OUT, grid=(1,), in_specs=[SC...  6.88 us
    pallas_call x1, Pallas kernels, combine_part(): pl.pallas_call(combine_kernel, out_shape=jax.ShapeDtypeStruct((4, 8, colu...  5.52 us
    all_to_all x4, waiting for transfers between devices, exchange(): lax.all_to_all(value, axis, split_axis=0, concat_axis=0, axis_index_group...  3.93 us
  transfers between devices with their start and end apart: 7, of which 3 were waited for; matrix products, arithmetic and copies ran while one was open for 4% of the time, Pallas kernels for 53%

profile of v2, /device:TPU:1, one launch (start us, length us, event | category | flops | bytes accessed | tf_op | source)
XLA Modules:
  0.0 83.0 jit_solution(4876521717441873914)
XLA Ops:
  0.6 1.3 %collective-permute-start = (bf16[1024,256]{1,0:T(8,128)(2,1)}, bf16[1024,256]{1,0:T(8,128)(2,1)S(1)}, u32[]{:S(2)}, u32[]{:S(2)}) collective-permute-start(bf16[1024,256]{1,0:T(8,128)(2,1)} %refs_1_.1), channel_id=1, source_target_pairs={{0,4},{1,5},{2,6},{3,7}} | collective-permute-start | bytes 1572872 | tf_op jit(solution)/shard_map/ppermute | solution.py:454
  1.9 1.3 %collective-permute-start.1 = (bf16[1024,256]{1,0:T(8,128)(2,1)}, bf16[1024,256]{1,0:T(8,128)(2,1)S(1)}, u32[]{:S(2)}, u32[]{:S(2)}) collective-permute-start(bf16[1024,256]{1,0:T(8,128)(2,1)} %refs_2_.1), channel_id=1, source_target_pairs={{0,4},{1,5},{2,6},{3,7}} | collective-permute-start | bytes 1572872 | tf_op jit(solution)/shard_map/ppermute | solution.py:455
  3.2 1.0 %slice.15 = bf16[1024,128]{1,0:T(8,128)(2,1)S(1)} slice(bf16[1024,256]{1,0:T(8,128)(2,1)} %refs_1_.1), slice={[0:1024], [0:128]} | slice | bytes 524288 | tf_op jit(solution)/shard_map/slice | solution.py:458
  4.2 1.0 %slice.16 = bf16[1024,128]{1,0:T(8,128)(2,1)S(1)} slice(bf16[1024,256]{1,0:T(8,128)(2,1)} %refs_2_.1), slice={[0:1024], [0:128]} | slice | bytes 524288 | tf_op jit(solution)/shard_map/slice | solution.py:458
  5.2 0.0 collective-permute-done
  5.2 1.1 %collective-permute-done.1 = bf16[1024,256]{1,0:T(8,128)(2,1)S(1)} collective-permute-done((bf16[1024,256]{1,0:T(8,128)(2,1)}, bf16[1024,256]{1,0:T(8,128)(2,1)S(1)}, u32[]{:S(2)}, u32[]{:S(2)}) %collective-permute-start.1) | collective-permute-done | bytes 524320 | tf_op jit(solution)/shard_map/ppermute | solution.py:455
  6.3 1.0 %maximum_select_fusion = bf16[16,64,256]{2,1,0:T(8,128)(2,1)} fusion(bf16[16,64,128]{2,1,0:T(8,128)(2,1)S(1)} %bitcast.18, bf16[16,64,128]{2,1,0:T(8,128)(2,1)S(1)} %bitcast.17, bf16[16,64,128]{2,1,0:T(8,128)(2,1)S(1)} %bitcast.20, bf16[16,64,128]{2,1,0:T(8,128)(2,1)S(1)} %bitcast.19, pred[]{:T(512)S(6)} %eq.3), kind=kLoop, calls=%fused_computation | loop fusion | flops 2359296 | bytes 1572865 | tf_op jit(solution)/shard_map/jit(_where)/select_n | solution.py:456
  7.3 6.4 %all-to-all-start = ((bf16[16,64,256]{2,1,0:T(8,128)(2,1)}), bf16[16,64,256]{2,1,0:T(8,128)(2,1)S(1)}, u32[]{:S(2)}, u32[]{:S(2)}) async-start(bf16[16,64,256]{2,1,0:T(8,128)(2,1)} %maximum_select_fusion), calls=%async_computation | async-start | bytes 1048576 | tf_op jit(solution)/shard_map/all_to_all | solution.py:437
  13.6 11.5 %question_block.1 = (bf16[256,1152]{1,0:T(8,128)(2,1)}, f32[8,1024]{1,0:T(8,128)}, f32[8,128]{1,0:T(8,128)}, f32[1024,512]{1,0:T(8,128)}, f32[1024,128]{1,0:T(8,128)}) custom-call(s32[1]{0:T(128)} %bitcast.1.place_ref, s32[256]{0:T(256)} %order_ref.1, bf16[256,1024]{1,0:T(8,128)(2,1)} %query_ref.3, bf16[1024,256]{1,0:T(8,128)(2,1)} %refs_1_.1, ...), custom_call_target="tpu_custom_call" | custom-call | flops 67108864 | bytes 262144 | tf_op jit(solution)/shard_map/question_block/pallas_call | solution.py:243
  25.1 0.0 all-to-all-done
  25.2 0.8 %broadcast_in_dim.2 = bf16[16,64,256]{2,1,0:T(8,128)(2,1)} broadcast(bf16[64,256]{1,0:T(8,128)(2,1)S(1)} %slice_bitcast_fusion), dimensions={1,2} | broadcast | bytes 557056 | tf_op jit(solution)/shard_map/broadcast_in_dim | solution.py:468
  26.0 6.7 %all-to-all-start.1 = ((bf16[16,64,256]{2,1,0:T(8,128)(2,1)}), bf16[16,64,256]{2,1,0:T(8,128)(2,1)S(1)}, u32[]{:S(2)}, u32[]{:S(2)}) async-start(bf16[16,64,256]{2,1,0:T(8,128)(2,1)} %broadcast_in_dim.2), calls=%async_computation.1 | async-start | bytes 1048576 | tf_op jit(solution)/shard_map/all_to_all | solution.py:437
  32.7 0.6 pad_add_fusion.place_ref
  33.3 6.9 %context_own.1 = (f32[1024,512]{1,0:T(8,128)}, f32[1024,128]{1,0:T(8,128)}) custom-call(s32[2]{0:T(128)} %pad_add_fusion.place_ref, bf16[1024,1024]{1,0:T(8,128)(2,1)} %query_ref.5, bf16[1024,256]{1,0:T(8,128)(2,1)} %refs_1_.1, bf16[1024,256]{1,0:T(8,128)(2,1)} %refs_2_.1), custom_call_target="tpu_custom_call" | custom-call | flops 67108864 | bytes 262144 | tf_op jit(solution)/shard_map/context_own/pallas_call | solution.py:158
  40.2 2.6 %all-to-all-done.1 = bf16[16,64,256]{2,1,0:T(8,128)(2,1)S(1)} async-done(((bf16[16,64,256]{2,1,0:T(8,128)(2,1)}), bf16[16,64,256]{2,1,0:T(8,128)(2,1)S(1)}, u32[]{:S(2)}, u32[]{:S(2)}) %all-to-all-start.1) | async-done | bytes 524320 | tf_op jit(solution)/shard_map/all_to_all | solution.py:437
  42.8 0.0 copy-start
  42.8 6.2 %all-to-all-start.2 = ((bf16[32,8,1152]{2,1,0:T(8,128)(2,1)}), bf16[32,8,1152]{2,1,0:T(8,128)(2,1)S(1)}, u32[]{:S(2)}, u32[]{:S(2)}) async-start(bf16[32,8,1152]{2,1,0:T(8,128)(2,1)} %bitcast.9), calls=%async_computation.2 | async-start | bytes 1179648 | tf_op jit(solution)/shard_map/all_to_all | solution.py:437
  49.0 0.3 collective-permute-start.2
  49.3 0.7 pad_add_fusion.1.place_ref
  49.9 0.0 copy-done
  50.0 10.0 %context_anchor.2.rest_0_ = bf16[1024,1024]{1,0:T(8,128)(2,1)} custom-call(s32[2]{0:T(128)} %pad_add_fusion.1.place_ref, bf16[1024,1024]{1,0:T(8,128)(2,1)} %query_ref.5, bf16[1024,256]{1,0:T(8,128)(2,1)} %bitcast.14, bf16[1024,256]{1,0:T(8,128)(2,1)} %bitcast.15, f32[1024,512]{1,0:T(8,128)} %get-tuple-element.23.sum_ref, f32[1024,128]{1,0:T(8,128)} %get-tuple-element.24.stat_ref), custom_call_target="tpu_custom_call" | custom-call | flops 67108864 | bytes 262144 | tf_op jit(solution)/shard_map/context_anchor/pallas_call | solution.py:413
  59.9 1.3 %all-to-all-done.2 = bf16[32,8,1152]{2,1,0:T(8,128)(2,1)S(1)} async-done(((bf16[32,8,1152]{2,1,0:T(8,128)(2,1)}), bf16[32,8,1152]{2,1,0:T(8,128)(2,1)S(1)}, u32[]{:S(2)}, u32[]{:S(2)}) %all-to-all-start.2) | async-done | bytes 589856 | tf_op jit(solution)/shard_map/all_to_all | solution.py:437
  61.2 0.0 copy-start.1
  61.2 0.8 %copy-done.1 = bf16[32,8,1152]{2,1,0:T(8,128)(2,1)} copy-done((bf16[32,8,1152]{2,1,0:T(8,128)(2,1)}, bf16[32,8,1152]{2,1,0:T(8,128)(2,1)S(1)}, u32[]{:S(2)}) %copy-start.1) | copy-done | bytes 589848
  62.1 5.5 %question_merge.1 = f32[4,8,1024]{2,1,0:T(8,128)} custom-call(bf16[256,1152]{1,0:T(8,128)(2,1)} %bitcast.16, f32[8,1024]{1,0:T(8,128)} %get-tuple-element.26.self_ref, f32[8,128]{1,0:T(8,128)} %get-tuple-element.17.self_lse_ref, bf16[1024,4096]{1,0:T(8,128)(2,1)} %weight_hbm.1), custom_call_target="tpu_custom_call" | custom-call | flops 67108864 | bytes 9437184 | tf_op jit(solution)/shard_map/question_merge/pallas_call | solution.py:331
  67.6 4.0 %all-to-all-start.3 = ((f32[4,8,1024]{2,1,0:T(8,128)}), f32[4,8,1024]{2,1,0:T(8,128)S(1)}, u32[]{:S(2)}, u32[]{:S(2)}) async-start(f32[4,8,1024]{2,1,0:T(8,128)} %question_merge.1), calls=%async_computation.3 | async-start | bytes 262144 | tf_op jit(solution)/shard_map/all_to_all | solution.py:437
  71.6 0.0 collective-permute-done.2.key_ref.value_ref
  71.6 0.0 copy-start.2
  71.6 0.8 copy-done.2
  72.4 10.0 %context_anchor.3 = bf16[1024,1024]{1,0:T(8,128)(2,1)} custom-call(s32[2]{0:T(128)} %pad_add_fusion.place_ref, bf16[1024,1024]{1,0:T(8,128)(2,1)} %query_ref.5, bf16[1024,256]{1,0:T(8,128)(2,1)} %copy-done.2, bf16[1024,256]{1,0:T(8,128)(2,1)} %copy-done.2, f32[1024,512]{1,0:T(8,128)} %get-tuple-element.28.sum_ref, ...), custom_call_target="tpu_custom_call", output_to_operand_aliasing={{}: (6, {})} | custom-call | flops 67108864 | bytes 262144 | tf_op jit(solution)/shard_map/context_anchor/pallas_call | solution.py:413
  82.4 0.0 all-to-all-done.3
  82.4 0.6 reduce_sum.9
  (3 shorter events, 0.0 us)
Async XLA Ops:
  0.6 4.6 %collective-permute-start = (bf16[1024,256]{1,0:T(8,128)(2,1)}, bf16[1024,256]{1,0:T(8,128)(2,1)S(1)}, u32[]{:S(2)}, u32[]{:S(2)}) collective-permute-start(bf16[1024,256]{1,0:T(8,128)(2,1)} %refs_1_.1), channel_id=1, source_target_pairs={{0,4},{1,5},{2,6},{3,7}} | collective-permute-start | bytes 1572872 | tf_op jit(solution)/shard_map/ppermute | solution.py:454
  1.9 4.3 %collective-permute-start.1 = (bf16[1024,256]{1,0:T(8,128)(2,1)}, bf16[1024,256]{1,0:T(8,128)(2,1)S(1)}, u32[]{:S(2)}, u32[]{:S(2)}) collective-permute-start(bf16[1024,256]{1,0:T(8,128)(2,1)} %refs_2_.1), channel_id=1, source_target_pairs={{0,4},{1,5},{2,6},{3,7}} | collective-permute-start | bytes 1572872 | tf_op jit(solution)/shard_map/ppermute | solution.py:455
  7.3 17.9 %all-to-all-start = ((bf16[16,64,256]{2,1,0:T(8,128)(2,1)}), bf16[16,64,256]{2,1,0:T(8,128)(2,1)S(1)}, u32[]{:S(2)}, u32[]{:S(2)}) async-start(bf16[16,64,256]{2,1,0:T(8,128)(2,1)} %maximum_select_fusion), calls=%async_computation | async-start | bytes 1048576 | tf_op jit(solution)/shard_map/all_to_all | solution.py:437
  26.0 16.8 %all-to-all-start.1 = ((bf16[16,64,256]{2,1,0:T(8,128)(2,1)}), bf16[16,64,256]{2,1,0:T(8,128)(2,1)S(1)}, u32[]{:S(2)}, u32[]{:S(2)}) async-start(bf16[16,64,256]{2,1,0:T(8,128)(2,1)} %broadcast_in_dim.2), calls=%async_computation.1 | async-start | bytes 1048576 | tf_op jit(solution)/shard_map/all_to_all | solution.py:437
  42.8 7.2 %copy-start = (bf16[16,64,256]{2,1,0:T(8,128)(2,1)}, bf16[16,64,256]{2,1,0:T(8,128)(2,1)S(1)}, u32[]{:S(2)}) copy-start(bf16[16,64,256]{2,1,0:T(8,128)(2,1)S(1)} %all-to-all-done.1) | copy-start | bytes 1572868
  42.8 18.4 %all-to-all-start.2 = ((bf16[32,8,1152]{2,1,0:T(8,128)(2,1)}), bf16[32,8,1152]{2,1,0:T(8,128)(2,1)S(1)}, u32[]{:S(2)}, u32[]{:S(2)}) async-start(bf16[32,8,1152]{2,1,0:T(8,128)(2,1)} %bitcast.9), calls=%async_computation.2 | async-start | bytes 1179648 | tf_op jit(solution)/shard_map/all_to_all | solution.py:437
  49.0 22.6 %collective-permute-start.2 = (bf16[1024,256]{1,0:T(8,128)(2,1)S(1)}, bf16[1024,256]{1,0:T(8,128)(2,1)S(1)}, u32[]{:S(2)}, u32[]{:S(2)}) collective-permute-start(bf16[1024,256]{1,0:T(8,128)(2,1)S(1)} %bitcast.13), channel_id=1, source_target_pairs={{0,4},{4,0},{8,12},{12,8},{16,20},{20,16},{24,28},{28,24},{32,36},... | collective-permute-start | bytes 1572872 | tf_op jit(solution)/shard_map/ppermute | solution.py:471
  61.2 0.8 %copy-start.1 = (bf16[32,8,1152]{2,1,0:T(8,128)(2,1)}, bf16[32,8,1152]{2,1,0:T(8,128)(2,1)S(1)}, u32[]{:S(2)}) copy-start(bf16[32,8,1152]{2,1,0:T(8,128)(2,1)S(1)} %all-to-all-done.2) | copy-start | bytes 1769476
  67.6 14.8 %all-to-all-start.3 = ((f32[4,8,1024]{2,1,0:T(8,128)}), f32[4,8,1024]{2,1,0:T(8,128)S(1)}, u32[]{:S(2)}, u32[]{:S(2)}) async-start(f32[4,8,1024]{2,1,0:T(8,128)} %question_merge.1), calls=%async_computation.3 | async-start | bytes 262144 | tf_op jit(solution)/shard_map/all_to_all | solution.py:437
  71.6 0.8 copy-start.2

commit v3 on v2

v3 whole, which is shorter than its diff:
```python
import math

import jax
import jax.numpy as jnp
from jax import lax
from jax.experimental import pallas as pl
from jax.experimental.pallas import tpu as pltpu
from jax.sharding import PartitionSpec as P

HEAD_DIM = 128
BLOCK = 1024
TILE = 256
QROWS = 256
GROUP = 4
HEADS = 8
EXTRA = 128
SCALE = math.log2(math.e) / math.sqrt(HEAD_DIM)
F32 = jnp.float32
BF16 = jnp.bfloat16
VMEM_LIMIT = 56 * 1024 * 1024
ANCHOR_ROWS = 512


def scores_of(queries, keys):
    return lax.dot_general(queries, keys, (((1,), (1,)), ((), ())), preferred_element_type=F32)


def weigh(scores):
    maxima = jnp.max(scores, axis=-1, keepdims=True)
    weights = jnp.exp2((scores - maxima) * SCALE)
    return maxima, weights, jnp.sum(weights, axis=-1, keepdims=True)


def whole(*shape):
    return pl.BlockSpec(shape, lambda step: (0,) * len(shape))


def columns_of(rows, width, at):
    return pl.BlockSpec((rows, width), lambda step: (0, at))


SCALARS = pl.BlockSpec(memory_space=pltpu.SMEM)


def times_values(weights, values):
    return jnp.dot(weights.astype(BF16), values, preferred_element_type=F32)


def head_cols(head):
    return slice(head * HEAD_DIM, (head + 1) * HEAD_DIM)


def staggered(items, scores_at, finish):
    scores = scores_at(items[0])
    for at, item in enumerate(items):
        later = scores_at(items[at + 1]) if at + 1 < len(items) else None
        finish(item, scores)
        scores = later


def question_kernel(
    place_ref,
    order_ref,
    query_ref,
    key_ref,
    value_ref,
    self_key_ref,
    self_value_ref,
    order_row_ref,
    out_ref,
    self_ref,
    self_lse_ref,
):
    lane = lax.broadcasted_iota(jnp.int32, (QROWS, EXTRA), 1)
    packed = [jnp.zeros((QROWS, EXTRA), F32)]
    first = pl.multiple_of((place_ref[2] // 2) * 16, 16)
    upper = place_ref[2] % 2 == 1
    row_ids = lax.broadcasted_iota(jnp.int32, (16, QROWS), 0)
    row_order = jnp.zeros((16, QROWS), jnp.int32)
    for row in range(16):
        row_order = jnp.where(row_ids == row, order_ref[first + row], row_order)
    allowed = jnp.concatenate([order_row_ref[...] <= row_order] * GROUP, axis=0)
    lse = jnp.zeros((8, EXTRA), F32)

    def scores_at(head):
        return scores_of(query_ref[:, head_cols(head)], key_ref[:, head_cols(head // GROUP)])

    def finish(head, scores):
        maxima, weights, totals = weigh(scores)
        summed = times_values(weights, value_ref[:, head_cols(head // GROUP)])
        out_ref[:, head_cols(head)] = (summed / totals).astype(BF16)
        packed[0] = jnp.where(lane == head, maxima * SCALE + jnp.log2(totals), packed[0])

    staggered(range(HEADS), scores_at, finish)
    rest, terms = packed[0], None
    for part in range(3):
        term = rest.astype(BF16).astype(F32)
        rest = rest - term
        terms = term if part == 0 else terms + pltpu.roll(term, part * HEADS, 1)
    out_ref[:, HEADS * HEAD_DIM :] = terms.astype(BF16)

    for kv in range(HEADS // GROUP):
        heads = range(kv * GROUP, (kv + 1) * GROUP)
        queries = jnp.concatenate(
            [query_ref[pl.ds(first, 16), head_cols(head)] for head in heads], axis=0
        )
        scores = scores_of(queries, self_key_ref[:, head_cols(kv)])
        maxima, weights, totals = weigh(jnp.where(allowed, scores, -jnp.inf))
        summed = times_values(weights, self_value_ref[:, head_cols(kv)]) / totals
        row_lse = maxima * SCALE + jnp.log2(totals)
        for at, head in enumerate(heads):
            low, high = slice(at * 16, at * 16 + 8), slice(at * 16 + 8, at * 16 + 16)
            self_ref[:, head_cols(head)] = jnp.where(upper, summed[high], summed[low])
            lse = jnp.where(lane[:8] == head, jnp.where(upper, row_lse[high], row_lse[low]), lse)
    self_lse_ref[...] = lse


def question_part(
    place, quest_query, ctx_key, ctx_value, quest_key, quest_value, quest_order
):
    rows, width = quest_query.shape
    return pl.pallas_call(
        question_kernel,
        out_shape=(
            jax.ShapeDtypeStruct((rows, width + EXTRA), BF16),
            jax.ShapeDtypeStruct((8, width), F32),
            jax.ShapeDtypeStruct((8, EXTRA), F32),
        ),
        grid=(1,),
        in_specs=[
            SCALARS,
            SCALARS,
            whole(rows, width),
            whole(*ctx_key.shape),
            whole(*ctx_value.shape),
            whole(*quest_key.shape),
            whole(*quest_value.shape),
            whole(1, QROWS),
        ],
        out_specs=(whole(rows, width + EXTRA), whole(8, width), whole(8, EXTRA)),
        compiler_params=pltpu.CompilerParams(vmem_limit_bytes=VMEM_LIMIT),
        cost_estimate=pl.CostEstimate(flops=1 << 26, bytes_accessed=1 << 18, transcendentals=1 << 16),
        name="question_block",
    )(
        place,
        quest_order,
        quest_query,
        ctx_key,
        ctx_value,
        quest_key,
        quest_value,
        quest_order.reshape(1, QROWS),
    )


def combine_kernel(
    parts_hbm, self_ref, self_lse_ref, weight_hbm, out_ref, parts_ref, weight_ref, sems
):
    step = out_ref.shape[2]
    arrived = pltpu.make_async_copy(parts_hbm, parts_ref, sems.at[4])
    arrived.start()
    loads = []
    for at in range(out_ref.shape[0]):
        cols = pl.ds(at * step, step)
        loads.append(
            pltpu.make_async_copy(weight_hbm.at[:, cols], weight_ref.at[:, cols], sems.at[at])
        )
        loads[-1].start()
    arrived.wait()
    blocks = parts_ref.shape[0] // 8
    width = HEADS * HEAD_DIM
    terms = parts_ref[:, width:].astype(F32)
    lse = terms + pltpu.roll(terms, EXTRA - HEADS, 1) + pltpu.roll(terms, EXTRA - 2 * HEADS, 1)
    lse = lse.reshape(blocks, 8, EXTRA)
    peak = jnp.maximum(jnp.max(lse, axis=0), self_lse_ref[...])
    scale = jnp.exp2(lse - peak[None])
    self_scale = jnp.exp2(self_lse_ref[...] - peak)
    inverse = 1.0 / (jnp.sum(scale, axis=0) + self_scale)
    scale = scale * inverse[None]
    self_scale = self_scale * inverse
    attended = []
    for head in range(HEADS):
        total = self_ref[:, head_cols(head)] * self_scale[:, head : head + 1]
        part = parts_ref[:, head_cols(head)].astype(F32).reshape(blocks, 8, HEAD_DIM)
        attended.append(total + jnp.sum(part * scale[:, :, head : head + 1], axis=0))
    attended = jnp.concatenate(attended, axis=1).astype(BF16)
    for at, load in enumerate(loads):
        load.wait()
        out_ref[at] = jnp.dot(
            attended, weight_ref[:, at * step : (at + 1) * step], preferred_element_type=F32
        )


def combine_part(parts, self_out, self_lse, out_weight):
    depth, columns = out_weight.shape
    return pl.pallas_call(
        combine_kernel,
        out_shape=jax.ShapeDtypeStruct((4, 8, columns // 4), F32),
        grid=(1,),
        in_specs=[
            pl.BlockSpec(memory_space=pltpu.HBM),
            whole(*self_out.shape),
            whole(*self_lse.shape),
            pl.BlockSpec(memory_space=pltpu.HBM),
        ],
        out_specs=whole(4, 8, columns // 4),
        scratch_shapes=[
            pltpu.VMEM(parts.shape, BF16),
            pltpu.VMEM((depth, columns), BF16),
            pltpu.SemaphoreType.DMA((5,)),
        ],
        compiler_params=pltpu.CompilerParams(vmem_limit_bytes=VMEM_LIMIT),
        cost_estimate=pl.CostEstimate(flops=2 * 8 * depth * columns, bytes_accessed=9 << 20, transcendentals=0),
        name="question_merge",
    )(parts, self_out, self_lse, out_weight)


def local_kernel(
    place_ref, query_ref, key_ref, value_ref, sum_out, stat_out, sum_ref, stat_ref, sems
):
    copies = []

    def send(source, target, rows):
        copy = pltpu.make_async_copy(source.at[rows], target.at[rows], sems.at[len(copies)])
        copy.start()
        copies.append(copy)

    row_ids = lax.broadcasted_iota(jnp.int32, (TILE, TILE), 0)
    col_ids = lax.broadcasted_iota(jnp.int32, (TILE, TILE), 1)
    causal = col_ids <= row_ids
    lane = lax.broadcasted_iota(jnp.int32, (TILE, EXTRA), 1)
    stats = {}

    def scores_at(item):
        tile, head = item
        rows = slice(tile * TILE, (tile + 1) * TILE)
        return scores_of(query_ref[rows, head_cols(head)], key_ref[: (tile + 1) * TILE, :])

    def finish(item, scores):
        tile, head = item
        rows = slice(tile * TILE, (tile + 1) * TILE)
        before = tile * TILE
        last = jnp.where(causal, scores[:, before:], -jnp.inf)
        scores = jnp.concatenate([scores[:, :before], last], axis=1) if before else last
        maxima, weights, totals = weigh(scores)
        values = value_ref[: before + TILE, :]
        sum_ref[rows, head_cols(head)] = times_values(weights, values)
        stat = stats.get(tile, jnp.zeros((TILE, EXTRA), F32))
        stat = jnp.where(lane == head, maxima, stat)
        stats[tile] = jnp.where(lane == GROUP + head, totals, stat)
        if head == GROUP - 1:
            stat_ref[rows, :] = stats[tile]
            send(sum_ref, sum_out, rows)
            send(stat_ref, stat_out, rows)

    tiles = range(BLOCK // TILE - 1, -1, -1)
    staggered([(tile, head) for tile in tiles for head in range(GROUP)], scores_at, finish)
    for copy in copies:
        copy.wait()


def local_part(turn, place, ctx_query, ctx_key, ctx_value):
    rows = ctx_query.shape[0]
    group = GROUP * HEAD_DIM
    at_head = lambda step, place: (0, place[turn])
    return pl.pallas_call(
        local_kernel,
        out_shape=(
            jax.ShapeDtypeStruct((rows, group), F32),
            jax.ShapeDtypeStruct((rows, EXTRA), F32),
        ),
        grid_spec=pltpu.PrefetchScalarGridSpec(
            num_scalar_prefetch=1,
            grid=(1,),
            in_specs=[
                pl.BlockSpec((rows, group), at_head),
                pl.BlockSpec((rows, HEAD_DIM), at_head),
                pl.BlockSpec((rows, HEAD_DIM), at_head),
            ],
            out_specs=(pl.BlockSpec(memory_space=pltpu.HBM),) * 2,
            scratch_shapes=[
                pltpu.VMEM((rows, group), F32),
                pltpu.VMEM((rows, EXTRA), F32),
                pltpu.SemaphoreType.DMA((2 * rows // TILE,)),
            ],
        ),
        compiler_params=pltpu.CompilerParams(vmem_limit_bytes=VMEM_LIMIT),
        cost_estimate=pl.CostEstimate(flops=1 << 26, bytes_accessed=1 << 18, transcendentals=1 << 16),
        name="context_own",
    )(place, ctx_query, ctx_key, ctx_value)


def anchor_kernel(place_ref, query_ref, *refs):
    out_ref, summed_ref = refs[-2:]
    is_anchor = place_ref[2] == 0
    lane = lax.broadcasted_iota(jnp.int32, (TILE, EXTRA), 1)

    def run(key_ref, value_ref, sum_ref, stat_ref):
        packed = {}

        def scores_at(item):
            row, head = item
            return scores_of(query_ref[row : row + TILE, head_cols(head)], key_ref[...])

        def finish(item, scores):
            row, head = item
            rows = slice(row, row + TILE)
            maxima, weights, totals = weigh(scores)
            summed_ref[rows, head_cols(head)] = times_values(weights, value_ref[...])
            all_maxima, all_totals = packed.get(row, (jnp.zeros((TILE, EXTRA), F32),) * 2)
            all_maxima = jnp.where(lane == head, maxima, all_maxima)
            all_totals = jnp.where(lane == head, totals, all_totals)
            packed[row] = all_maxima, all_totals
            if head == GROUP - 1:
                merge(rows, all_maxima, all_totals)

        def merge(rows, maxima, totals):
            own_max = stat_ref[rows, :]
            own_total = pltpu.roll(own_max, EXTRA - GROUP, 1)
            maxima = jnp.where(is_anchor, -jnp.inf, maxima)
            peak = jnp.maximum(maxima, own_max)
            scale = jnp.exp2((maxima - peak) * SCALE)
            own_scale = jnp.exp2((own_max - peak) * SCALE)
            inverse = 1.0 / (totals * scale + own_total * own_scale)
            scale, own_scale = scale * inverse, own_scale * inverse
            for head in range(GROUP):
                cols = head_cols(head)
                out_ref[rows, cols] = (
                    summed_ref[rows, cols] * scale[:, head : head + 1]
                    + sum_ref[rows, cols] * own_scale[:, head : head + 1]
                ).astype(BF16)

        rows = range(0, ANCHOR_ROWS, TILE)
        staggered([(row, head) for row in rows for head in range(GROUP)], scores_at, finish)

    @pl.when(pl.program_id(0) == 0)
    def _():
        run(*refs[:4])

    @pl.when(pl.program_id(0) == 1)
    def _():
        run(*refs[4:8])


def anchor_part(place, ctx_query, here, own_here, there, own_there):
    rows, width = ctx_query.shape
    group = GROUP * HEAD_DIM
    last = rows // ANCHOR_ROWS - 1
    tile_of = lambda turn, tile, place: (tile, place[turn])
    first_turn = lambda turn, tile, place: (jnp.where(turn == 0, tile, last), 0)
    second_turn = lambda turn, tile, place: (jnp.where(turn == 0, 0, tile), 0)
    keys = pl.BlockSpec((BLOCK, HEAD_DIM), lambda turn, tile, place: (0, 0))
    values = pl.BlockSpec((BLOCK, HEAD_DIM), lambda turn, tile, place: (0, 1))
    in_specs = [pl.BlockSpec((ANCHOR_ROWS, group), tile_of)]
    for row_of in (first_turn, second_turn):
        in_specs += [keys, values]
        in_specs += [pl.BlockSpec((ANCHOR_ROWS, columns), row_of) for columns in (group, EXTRA)]
    return pl.pallas_call(
        anchor_kernel,
        out_shape=jax.ShapeDtypeStruct((rows, width), BF16),
        grid_spec=pltpu.PrefetchScalarGridSpec(
            num_scalar_prefetch=1,
            grid=(2, rows // ANCHOR_ROWS),
            in_specs=in_specs,
            out_specs=pl.BlockSpec((ANCHOR_ROWS, group), tile_of),
            scratch_shapes=[pltpu.VMEM((ANCHOR_ROWS, group), F32)],
        ),
        compiler_params=pltpu.CompilerParams(vmem_limit_bytes=VMEM_LIMIT),
        cost_estimate=pl.CostEstimate(flops=1 << 31, bytes_accessed=1 << 20, transcendentals=1 << 16),
        name="context_anchor",
    )(place, ctx_query, here, here, *own_here, there, there, *own_there)


def after(value, *others):
    return lax.optimization_barrier((value, *others))[0]


def device_at(z, y, core):
    return (z * 4 + y) * 2 + core


def edges(phase, steps):
    pairs = []
    for core in range(2):
        for first, last in steps:
            for other in range(1 if phase == 0 else 4):
                along_y = (core == 0) == (phase == 0)
                ends = [
                    device_at(other, at, core) if along_y else device_at(at, other, core)
                    for at in (first, last)
                ]
                pairs.append(tuple(ends))
    return pairs


def exchange(value, axis):
    return lax.all_to_all(value, axis, split_axis=0, concat_axis=0, tiled=True)


def per_device(
    ctx_query, ctx_key, ctx_value, quest_query, quest_key, quest_value, quest_order, out_weight
):
    me = lax.axis_index("ctx").astype(jnp.int32)
    devices = lax.axis_size("ctx")
    core = lax.rem(me, 2)
    place = jnp.stack([core, 1 - core, me])
    siblings = [(at, at ^ 1) for at in range(devices)]

    def head_of(at):
        cols = slice(at * HEAD_DIM, (at + 1) * HEAD_DIM)
        return jnp.concatenate([ctx_key[:, cols], ctx_value[:, cols]], axis=1)

    def send(value, *steps):
        return lax.ppermute(value, "ctx", edges(*steps))

    moved = lax.ppermute(head_of(1), "ctx", [(0, 1)])
    half = jnp.where(me == 0, head_of(0), moved)
    moved = send(half, 0, [(0, 1)])
    parts, self_out, self_lse = question_part(
        place, quest_query, ctx_key, ctx_value, quest_key, quest_value, quest_order
    )
    half = half + after(moved, self_lse)
    moved = send(half, 0, [(0, 3), (1, 2)])
    width = parts.shape[1]
    parts = exchange(after(parts, half).reshape(devices, -1, width), "ctx").reshape(QROWS, width)
    own_here = local_part(0, place, after(ctx_query, half), ctx_key, ctx_value)
    half = half + after(moved, own_here[1])
    moved = send(half, 1, [(0, 1)])
    own_there = local_part(1, place, after(ctx_query, half), ctx_key, ctx_value)
    half = half + after(moved, own_there[1])
    moved = send(half, 1, [(0, 3), (1, 2)])
    projected = combine_part(after(parts, half), self_out, self_lse, out_weight)
    half = half + after(moved, projected)
    other_half = lax.ppermute(half, "ctx", siblings)
    projected = exchange(after(projected, half), "head")
    ctx_out = anchor_part(place, ctx_query, half, own_here, other_half, own_there)
    answer = jnp.sum(after(projected, ctx_out), axis=0).astype(BF16)
    return (ctx_out, answer)


def solution(mesh):
    in_specs = (
        P("ctx", "head"),
        P("ctx", "head"),
        P("ctx", "head"),
        P(None, "head"),
        P(None, "head"),
        P(None, "head"),
        P(),
        P("head", None),
    )
    out_specs = (P("ctx", "head"), P("ctx", "head"))
    return jax.shard_map(
        per_device, mesh=mesh, in_specs=in_specs, out_specs=out_specs, check_vma=False
    )
```

time: 83.8 us -> 73.5 us (0.88)
  starting transfers between devices: 26.1 us -> 22.3 us
  Pallas kernels: 43.8 us -> 41 us
  local copies, waits for them, and re-layouts: 4.46 us -> 2.89 us
  waiting for transfers between devices: 4.99 us -> 3.95 us
    all_to_all x4 -> x2, starting transfers between devices: 23.2 us -> 10.8 us  [exchange(): return lax.all_to_all(value, axis, split_axis=0, concat_axis=0, tiled=True)]
    ppermute x2 -> x5, starting transfers between devices: 2.58 us -> 10.9 us  [the longest x4 9.64 us: send(): return lax.ppermute(value, 'ctx', edges(*steps))]
    pallas_call x1, Pallas kernels: 11.5 us -> 5.36 us  [question_part(): pl.pallas_call(question_kernel, out_shape=(jax.ShapeDtypeStruct((rows, wi...]
    pallas_call x1 -> x2, Pallas kernels: 6.88 us -> 12.9 us  [local_part(): pl.pallas_call(local_kernel, out_shape=(jax.ShapeDtypeStruct((rows, group...]
    all_to_all x4 -> x2, waiting for transfers between devices: 3.93 us -> 1.09 us  [exchange(): return lax.all_to_all(value, axis, split_axis=0, concat_axis=0, tiled=True)]
    pallas_call x2 -> x1, Pallas kernels: 19.9 us -> 17.2 us  [anchor_part(): pl.pallas_call(anchor_kernel, out_shape=jax.ShapeDtypeStruct((rows, width...]
    ppermute x2 -> x5, waiting for transfers between devices: 1.05 us -> 2.86 us  [the longest x1 2.79 us: per_device(): moved = lax.ppermute(head_of(1), 'ctx', [(0, 1)])]
    broadcast_in_dim x1 -> x0, local copies, waits for them, and re-layouts: 0.84 us -> none  [per_device(): jnp.broadcast_to(shares[None], (chips, *shares.shape))]
  transfers between devices with their start and end apart: 7 -> 8, of which waited for: 3 -> 3; matrix products, arithmetic and copies ran while one was open for 4% -> 1% of each run, Pallas kernels for 53% -> 56%
where the time goes in v3:
time: 73.5 us; the launch traced here: 72.9 us
  Pallas kernels  41 us (56%)
  starting transfers between devices  22.3 us (30%)
  waiting for transfers between devices  3.95 us (5%)
  local copies, waits for them, and re-layouts  2.89 us (4%)
  other arithmetic  2.02 us (3%)
  between operations  0.8 us (1%)
    pallas_call x1, Pallas kernels, anchor_part(): pl.pallas_call(anchor_kernel, out_shape=jax.ShapeDtypeStruct((rows, width...  17.2 us
    pallas_call x2, Pallas kernels, local_part(): pl.pallas_call(local_kernel, out_shape=(jax.ShapeDtypeStruct((rows, group...  12.9 us
    all_to_all x2, starting transfers between devices, exchange(): return lax.all_to_all(value, axis, split_axis=0, concat_axis=0, tiled=True)  10.8 us
    ppermute x4, starting transfers between devices, send(): return lax.ppermute(value, 'ctx', edges(*steps))  9.64 us
    pallas_call x1, Pallas kernels, combine_part(): pl.pallas_call(combine_kernel, out_shape=jax.ShapeDtypeStruct((4, 8, colu...  5.5 us
    pallas_call x1, Pallas kernels, question_part(): pl.pallas_call(question_kernel, out_shape=(jax.ShapeDtypeStruct((rows, wi...  5.36 us
    ppermute x1, waiting for transfers between devices, per_device(): moved = lax.ppermute(head_of(1), 'ctx', [(0, 1)])  2.79 us
    unnamed x6, local copies, waits for them, and re-layouts  1.62 us
  transfers between devices with their start and end apart: 8, of which 3 were waited for; matrix products, arithmetic and copies ran while one was open for 1% of the time, Pallas kernels for 56%

profile of v3, /device:TPU:1, one launch (start us, length us, event | category | flops | bytes accessed | tf_op | source)
XLA Modules:
  0.0 72.9 jit_solution(3313715425134250638)
XLA Ops:
  0.6 1.3 %fusion = (bf16[1024,128]{1,0:T(8,128)(2,1)S(1)}, bf16[1024,128]{1,0:T(8,128)(2,1)S(1)}, bf16[1024,128]{1,0:T(8,128)(2,1)S(1)}, bf16[1024,128]{1,0:T(8,128)(2,1)S(1)}) fusion(bf16[1024,256]{1,0:T(8,128)(2,1)} %key_ref.5, bf16[1024,256]{1,0:T(8,128)(2,1)} %value_ref.5), kind=kLoop, calls=%fused_computation.3 | loop fusion | bytes 2097152 | tf_op jit(solution)/shard_map/slice | solution.py:411
  1.9 0.1 pad_maximum_fusion
  2.0 1.3 %collective-permute-start = (bf16[1024,256]{1,0:T(8,128)(2,1)S(1)}, bf16[1024,256]{1,0:T(8,128)(2,1)S(1)}, u32[]{:S(2)}, u32[]{:S(2)}) collective-permute-start(bf16[1024,256]{1,0:T(8,128)(2,1)S(1)} %pad_maximum_fusion), channel_id=1, source_target_pairs={{0,4},{1,5},{2,6},{3,7}} | collective-permute-start | bytes 1572872 | tf_op jit(solution)/shard_map/ppermute | solution.py:416
  3.3 2.8 %collective-permute-done = bf16[1024,256]{1,0:T(8,128)(2,1)S(1)} collective-permute-done((bf16[1024,256]{1,0:T(8,128)(2,1)S(1)}, bf16[1024,256]{1,0:T(8,128)(2,1)S(1)}, u32[]{:S(2)}, u32[]{:S(2)}) %collective-permute-start) | collective-permute-done | bytes 524320 | tf_op jit(solution)/shard_map/ppermute | solution.py:416
  6.1 0.2 maximum_select_fusion
  6.2 1.3 %collective-permute-start.1 = (bf16[1024,256]{1,0:T(8,128)(2,1)S(1)}, bf16[1024,256]{1,0:T(8,128)(2,1)S(1)}, u32[]{:S(2)}, u32[]{:S(2)}) collective-permute-start(bf16[1024,256]{1,0:T(8,128)(2,1)S(1)} %maximum_select_fusion), channel_id=1, source_target_pairs={{0,8},{4,36},{1,9},{5,37},{2,10},{6,38},{3,11},{7,39}} | collective-permute-start | bytes 1572872 | tf_op jit(solution)/shard_map/ppermute | solution.py:414
  7.6 0.7 pad_add_fusion.place_ref
  8.2 5.4 %question_block.1 = (bf16[256,1152]{1,0:T(8,128)(2,1)}, f32[8,1024]{1,0:T(8,128)}, f32[8,128]{1,0:T(8,128)}) custom-call(s32[3]{0:T(128)} %pad_add_fusion.place_ref, s32[256]{0:T(256)} %order_ref.1, bf16[256,1024]{1,0:T(8,128)(2,1)} %query_ref.2, bf16[1024,256]{1,0:T(8,128)(2,1)} %key_ref.5, bf16[1024,256]{1,0:T(8,128)(2,1)} %value_ref.5, ...), custom_call_target="tpu_custom_call" | custom-call | flops 67108864 | bytes 262144 | tf_op jit(solution)/shard_map/question_block/pallas_call | solution.py:122
  13.6 0.1 collective-permute-done.1
  13.6 0.1 add.12
  13.8 2.5 %collective-permute-start.2 = (bf16[1024,256]{1,0:T(8,128)(2,1)S(1)}, bf16[1024,256]{1,0:T(8,128)(2,1)S(1)}, u32[]{:S(2)}, u32[]{:S(2)}) collective-permute-start(bf16[1024,256]{1,0:T(8,128)(2,1)S(1)} %add.12), channel_id=1, source_target_pairs={{0,24},{8,16},{4,100},{36,68},{1,25},{9,17},{5,101},{37,69},{2,26}... | collective-permute-start | bytes 1572872 | tf_op jit(solution)/shard_map/ppermute | solution.py:414
  16.2 6.4 %context_own.2 = (f32[1024,512]{1,0:T(8,128)}, f32[1024,128]{1,0:T(8,128)}) custom-call(s32[3]{0:T(128)} %pad_add_fusion.place_ref, bf16[1024,1024]{1,0:T(8,128)(2,1)} %query_ref.5, bf16[1024,256]{1,0:T(8,128)(2,1)} %key_ref.5, bf16[1024,256]{1,0:T(8,128)(2,1)} %value_ref.5), custom_call_target="tpu_custom_call" | custom-call | flops 67108864 | bytes 262144 | tf_op jit(solution)/shard_map/context_own/pallas_call | solution.py:266
  22.7 0.0 collective-permute-done.2
  22.7 0.1 add.13
  22.8 1.3 %collective-permute-start.3 = (bf16[1024,256]{1,0:T(8,128)(2,1)S(1)}, bf16[1024,256]{1,0:T(8,128)(2,1)S(1)}, u32[]{:S(2)}, u32[]{:S(2)}) collective-permute-start(bf16[1024,256]{1,0:T(8,128)(2,1)S(1)} %add.13), channel_id=1, source_target_pairs={{0,32},{8,40},{16,48},{24,56},{4,12},{36,44},{68,76},{100,108},{1,... | collective-permute-start | bytes 1572872 | tf_op jit(solution)/shard_map/ppermute | solution.py:414
  24.2 6.4 %all-to-all-start = ((bf16[32,8,1152]{2,1,0:T(8,128)(2,1)}), bf16[32,8,1152]{2,1,0:T(8,128)(2,1)S(1)}, u32[]{:S(2)}, u32[]{:S(2)}) async-start(bf16[32,8,1152]{2,1,0:T(8,128)(2,1)} %bitcast.4), calls=%async_computation | async-start | bytes 1179648 | tf_op jit(solution)/shard_map/all_to_all | solution.py:397
  30.6 6.5 %context_own.3 = (f32[1024,512]{1,0:T(8,128)}, f32[1024,128]{1,0:T(8,128)}) custom-call(s32[3]{0:T(128)} %pad_add_fusion.place_ref, bf16[1024,1024]{1,0:T(8,128)(2,1)} %query_ref.5, bf16[1024,256]{1,0:T(8,128)(2,1)} %key_ref.5, bf16[1024,256]{1,0:T(8,128)(2,1)} %value_ref.5), custom_call_target="tpu_custom_call" | custom-call | flops 67108864 | bytes 262144 | tf_op jit(solution)/shard_map/context_own/pallas_call | solution.py:266
  37.0 0.0 collective-permute-done.3
  37.0 0.1 add.14
  37.2 4.5 %collective-permute-start.4 = (bf16[1024,256]{1,0:T(8,128)(2,1)S(1)}, bf16[1024,256]{1,0:T(8,128)(2,1)S(1)}, u32[]{:S(2)}, u32[]{:S(2)}) collective-permute-start(bf16[1024,256]{1,0:T(8,128)(2,1)S(1)} %add.14), channel_id=1, source_target_pairs={{0,96},{8,104},{16,112},{24,120},{32,64},{40,72},{48,80},{56,88},{... | collective-permute-start | bytes 1572872 | tf_op jit(solution)/shard_map/ppermute | solution.py:414
  41.7 1.1 %all-to-all-done = bf16[32,8,1152]{2,1,0:T(8,128)(2,1)S(1)} async-done(((bf16[32,8,1152]{2,1,0:T(8,128)(2,1)}), bf16[32,8,1152]{2,1,0:T(8,128)(2,1)S(1)}, u32[]{:S(2)}, u32[]{:S(2)}) %all-to-all-start) | async-done | bytes 589856 | tf_op jit(solution)/shard_map/all_to_all | solution.py:397
  42.8 0.8 %copy-done.1 = bf16[32,8,1152]{2,1,0:T(8,128)(2,1)} copy-done((bf16[32,8,1152]{2,1,0:T(8,128)(2,1)}, bf16[32,8,1152]{2,1,0:T(8,128)(2,1)S(1)}, u32[]{:S(2)}) %copy-start.1) | copy-done | bytes 589848
  43.6 5.5 %question_merge.1 = f32[4,8,1024]{2,1,0:T(8,128)} custom-call(bf16[256,1152]{1,0:T(8,128)(2,1)} %bitcast.6, f32[8,1024]{1,0:T(8,128)} %get-tuple-element.30.self_ref, f32[8,128]{1,0:T(8,128)} %get-tuple-element.19.self_lse_ref, bf16[1024,4096]{1,0:T(8,128)(2,1)} %weight_hbm.1), custom_call_target="tpu_custom_call" | custom-call | flops 67108864 | bytes 9437184 | tf_op jit(solution)/shard_map/question_merge/pallas_call | solution.py:196
  49.1 0.0 collective-permute-done.4
  49.1 0.1 add.15.refs_0_.refs_1_
  49.3 0.6 collective-permute-start.5
  49.9 4.4 %all-to-all-start.1 = ((f32[4,8,1024]{2,1,0:T(8,128)}), f32[4,8,1024]{2,1,0:T(8,128)S(1)}, u32[]{:S(2)}, u32[]{:S(2)}) async-start(f32[4,8,1024]{2,1,0:T(8,128)} %question_merge.1), calls=%async_computation.1 | async-start | bytes 262144 | tf_op jit(solution)/shard_map/all_to_all | solution.py:397
  54.3 0.0 collective-permute-done.5.refs_4_.refs_5_
  54.3 0.8 %copy-done.2 = bf16[1024,256]{1,0:T(8,128)(2,1)} copy-done((bf16[1024,256]{1,0:T(8,128)(2,1)}, bf16[1024,256]{1,0:T(8,128)(2,1)S(1)}, u32[]{:S(2)}) %copy-start.2) | copy-done | bytes 524312
  55.1 17.2 %context_anchor.1 = bf16[1024,1024]{1,0:T(8,128)(2,1)} custom-call(s32[3]{0:T(128)} %pad_add_fusion.place_ref, bf16[1024,1024]{1,0:T(8,128)(2,1)} %query_ref.5, bf16[1024,256]{1,0:T(8,128)(2,1)} %copy-done, bf16[1024,256]{1,0:T(8,128)(2,1)} %copy-done, f32[1024,512]{1,0:T(8,128)} %get-tuple-element.32.refs_2_, f32[1024,128]{1,0:T(8,128)} %get-tuple-element.22.refs_3_, ...), custom_call_target="tpu_custom_call" | custom-call | flops 2147483648 | bytes 1048576 | tf_op jit(solution)/shard_map/context_anchor/pallas_call | solution.py:358
  72.3 0.0 all-to-all-done.1
  72.3 0.6 reduce_sum.9
  (4 shorter events, 0.0 us)
Async XLA Ops:
  2.0 4.1 %collective-permute-start = (bf16[1024,256]{1,0:T(8,128)(2,1)S(1)}, bf16[1024,256]{1,0:T(8,128)(2,1)S(1)}, u32[]{:S(2)}, u32[]{:S(2)}) collective-permute-start(bf16[1024,256]{1,0:T(8,128)(2,1)S(1)} %pad_maximum_fusion), channel_id=1, source_target_pairs={{0,4},{1,5},{2,6},{3,7}} | collective-permute-start | bytes 1572872 | tf_op jit(solution)/shard_map/ppermute | solution.py:416
  6.2 7.4 %collective-permute-start.1 = (bf16[1024,256]{1,0:T(8,128)(2,1)S(1)}, bf16[1024,256]{1,0:T(8,128)(2,1)S(1)}, u32[]{:S(2)}, u32[]{:S(2)}) collective-permute-start(bf16[1024,256]{1,0:T(8,128)(2,1)S(1)} %maximum_select_fusion), channel_id=1, source_target_pairs={{0,8},{4,36},{1,9},{5,37},{2,10},{6,38},{3,11},{7,39}} | collective-permute-start | bytes 1572872 | tf_op jit(solution)/shard_map/ppermute | solution.py:414
  13.8 8.9 %collective-permute-start.2 = (bf16[1024,256]{1,0:T(8,128)(2,1)S(1)}, bf16[1024,256]{1,0:T(8,128)(2,1)S(1)}, u32[]{:S(2)}, u32[]{:S(2)}) collective-permute-start(bf16[1024,256]{1,0:T(8,128)(2,1)S(1)} %add.12), channel_id=1, source_target_pairs={{0,24},{8,16},{4,100},{36,68},{1,25},{9,17},{5,101},{37,69},{2,26}... | collective-permute-start | bytes 1572872 | tf_op jit(solution)/shard_map/ppermute | solution.py:414
  22.8 14.2 %collective-permute-start.3 = (bf16[1024,256]{1,0:T(8,128)(2,1)S(1)}, bf16[1024,256]{1,0:T(8,128)(2,1)S(1)}, u32[]{:S(2)}, u32[]{:S(2)}) collective-permute-start(bf16[1024,256]{1,0:T(8,128)(2,1)S(1)} %add.13), channel_id=1, source_target_pairs={{0,32},{8,40},{16,48},{24,56},{4,12},{36,44},{68,76},{100,108},{1,... | collective-permute-start | bytes 1572872 | tf_op jit(solution)/shard_map/ppermute | solution.py:414
  24.2 18.6 %all-to-all-start = ((bf16[32,8,1152]{2,1,0:T(8,128)(2,1)}), bf16[32,8,1152]{2,1,0:T(8,128)(2,1)S(1)}, u32[]{:S(2)}, u32[]{:S(2)}) async-start(bf16[32,8,1152]{2,1,0:T(8,128)(2,1)} %bitcast.4), calls=%async_computation | async-start | bytes 1179648 | tf_op jit(solution)/shard_map/all_to_all | solution.py:397
  37.2 12.0 %collective-permute-start.4 = (bf16[1024,256]{1,0:T(8,128)(2,1)S(1)}, bf16[1024,256]{1,0:T(8,128)(2,1)S(1)}, u32[]{:S(2)}, u32[]{:S(2)}) collective-permute-start(bf16[1024,256]{1,0:T(8,128)(2,1)S(1)} %add.14), channel_id=1, source_target_pairs={{0,96},{8,104},{16,112},{24,120},{32,64},{40,72},{48,80},{56,88},{... | collective-permute-start | bytes 1572872 | tf_op jit(solution)/shard_map/ppermute | solution.py:414
  42.8 0.8 %copy-start.1 = (bf16[32,8,1152]{2,1,0:T(8,128)(2,1)}, bf16[32,8,1152]{2,1,0:T(8,128)(2,1)S(1)}, u32[]{:S(2)}) copy-start(bf16[32,8,1152]{2,1,0:T(8,128)(2,1)S(1)} %all-to-all-done) | copy-start | bytes 1769476
  49.3 5.0 %copy-start = (bf16[1024,256]{1,0:T(8,128)(2,1)}, bf16[1024,256]{1,0:T(8,128)(2,1)S(1)}, u32[]{:S(2)}) copy-start(bf16[1024,256]{1,0:T(8,128)(2,1)S(1)} %add.15.refs_0_.refs_1_) | copy-start | bytes 1572868
  49.3 5.0 %collective-permute-start.5 = (bf16[1024,256]{1,0:T(8,128)(2,1)S(1)}, bf16[1024,256]{1,0:T(8,128)(2,1)S(1)}, u32[]{:S(2)}, u32[]{:S(2)}) collective-permute-start(bf16[1024,256]{1,0:T(8,128)(2,1)S(1)} %add.15.refs_0_.refs_1_), channel_id=1, source_target_pairs={{0,4},{4,0},{8,12},{12,8},{16,20},{20,16},{24,28},{28,24},{32,36},... | collective-permute-start | bytes 1572872 | tf_op jit(solution)/shard_map/ppermute | solution.py:434
  49.9 22.4 %all-to-all-start.1 = ((f32[4,8,1024]{2,1,0:T(8,128)}), f32[4,8,1024]{2,1,0:T(8,128)S(1)}, u32[]{:S(2)}, u32[]{:S(2)}) async-start(f32[4,8,1024]{2,1,0:T(8,128)} %question_merge.1), calls=%async_computation.1 | async-start | bytes 262144 | tf_op jit(solution)/shard_map/all_to_all | solution.py:397
  54.3 0.8 %copy-start.2 = (bf16[1024,256]{1,0:T(8,128)(2,1)}, bf16[1024,256]{1,0:T(8,128)(2,1)S(1)}, u32[]{:S(2)}) copy-start(bf16[1024,256]{1,0:T(8,128)(2,1)S(1)} %collective-permute-done.5.refs_4_.refs_5_) | copy-start | bytes 1572868

commit v4 on v3

--- a/solution.py
+++ b/solution.py
@@ -154,11 +154,25 @@
 
 
 def combine_kernel(
-    parts_hbm, self_ref, self_lse_ref, weight_hbm, out_ref, parts_ref, weight_ref, sems
+    parts_hbm,
+    self_hbm,
+    self_lse_hbm,
+    weight_hbm,
+    out_ref,
+    parts_ref,
+    self_ref,
+    self_lse_ref,
+    weight_ref,
+    sems,
 ):
     step = out_ref.shape[2]
-    arrived = pltpu.make_async_copy(parts_hbm, parts_ref, sems.at[4])
-    arrived.start()
+    arrived = [
+        pltpu.make_async_copy(parts_hbm, parts_ref, sems.at[4]),
+        pltpu.make_async_copy(self_hbm, self_ref, sems.at[5]),
+        pltpu.make_async_copy(self_lse_hbm, self_lse_ref, sems.at[6]),
+    ]
+    for copy in arrived:
+        copy.start()
     loads = []
     for at in range(out_ref.shape[0]):
         cols = pl.ds(at * step, step)
@@ -166,7 +180,8 @@
             pltpu.make_async_copy(weight_hbm.at[:, cols], weight_ref.at[:, cols], sems.at[at])
         )
         loads[-1].start()
-    arrived.wait()
+    for copy in arrived:
+        copy.wait()
     blocks = parts_ref.shape[0] // 8
     width = HEADS * HEAD_DIM
     terms = parts_ref[:, width:].astype(F32)
@@ -199,15 +214,17 @@
         grid=(1,),
         in_specs=[
             pl.BlockSpec(memory_space=pltpu.HBM),
-            whole(*self_out.shape),
-            whole(*self_lse.shape),
+            pl.BlockSpec(memory_space=pltpu.HBM),
+            pl.BlockSpec(memory_space=pltpu.HBM),
             pl.BlockSpec(memory_space=pltpu.HBM),
         ],
         out_specs=whole(4, 8, columns // 4),
         scratch_shapes=[
             pltpu.VMEM(parts.shape, BF16),
+            pltpu.VMEM(self_out.shape, F32),
+            pltpu.VMEM(self_lse.shape, F32),
             pltpu.VMEM((depth, columns), BF16),
-            pltpu.SemaphoreType.DMA((5,)),
+            pltpu.SemaphoreType.DMA((7,)),
         ],
         compiler_params=pltpu.CompilerParams(vmem_limit_bytes=VMEM_LIMIT),
         cost_estimate=pl.CostEstimate(flops=2 * 8 * depth * columns, bytes_accessed=9 << 20, transcendentals=0),

time: 73.5 us -> 72.9 us (level)
  no operation moved by 1% of the time
where the time goes in v4:
time: 72.9 us; the launch traced here: 72.3 us
  Pallas kernels  40.3 us (55%)
  starting transfers between devices  22.4 us (31%)
  waiting for transfers between devices  3.95 us (5%)
  local copies, waits for them, and re-layouts  2.89 us (4%)
  other arithmetic  2.02 us (3%)
  between operations  0.8 us (1%)
    pallas_call x1, Pallas kernels, anchor_part(): pl.pallas_call(anchor_kernel, out_shape=jax.ShapeDtypeStruct((rows, width...  17.2 us
    pallas_call x2, Pallas kernels, local_part(): pl.pallas_call(local_kernel, out_shape=(jax.ShapeDtypeStruct((rows, group...  12.9 us
    all_to_all x2, starting transfers between devices, exchange(): return lax.all_to_all(value, axis, split_axis=0, concat_axis=0, tiled=True)  10.8 us
    ppermute x4, starting transfers between devices, send(): return lax.ppermute(value, 'ctx', edges(*steps))  9.64 us
    pallas_call x1, Pallas kernels, question_part(): pl.pallas_call(question_kernel, out_shape=(jax.ShapeDtypeStruct((rows, wi...  5.36 us
    pallas_call x1, Pallas kernels, combine_part(): pl.pallas_call(combine_kernel, out_shape=jax.ShapeDtypeStruct((4, 8, colu...  4.79 us
    ppermute x1, waiting for transfers between devices, per_device(): moved = lax.ppermute(head_of(1), 'ctx', [(0, 1)])  2.79 us
    unnamed x6, local copies, waits for them, and re-layouts  1.62 us
  transfers between devices with their start and end apart: 8, of which 3 were waited for; matrix products, arithmetic and copies ran while one was open for 1% of the time, Pallas kernels for 56%

profile of v4, /device:TPU:1, one launch (start us, length us, event | category | flops | bytes accessed | tf_op | source)
XLA Modules:
  0.0 72.3 jit_solution(5346254940315988730)
XLA Ops:
  0.6 1.3 %fusion = (bf16[1024,128]{1,0:T(8,128)(2,1)S(1)}, bf16[1024,128]{1,0:T(8,128)(2,1)S(1)}, bf16[1024,128]{1,0:T(8,128)(2,1)S(1)}, bf16[1024,128]{1,0:T(8,128)(2,1)S(1)}) fusion(bf16[1024,256]{1,0:T(8,128)(2,1)} %key_ref.5, bf16[1024,256]{1,0:T(8,128)(2,1)} %value_ref.5), kind=kLoop, calls=%fused_computation.3 | loop fusion | bytes 2097152 | tf_op jit(solution)/shard_map/slice | solution.py:428
  1.9 0.1 pad_maximum_fusion
  2.0 1.3 %collective-permute-start = (bf16[1024,256]{1,0:T(8,128)(2,1)S(1)}, bf16[1024,256]{1,0:T(8,128)(2,1)S(1)}, u32[]{:S(2)}, u32[]{:S(2)}) collective-permute-start(bf16[1024,256]{1,0:T(8,128)(2,1)S(1)} %pad_maximum_fusion), channel_id=1, source_target_pairs={{0,4},{1,5},{2,6},{3,7}} | collective-permute-start | bytes 1572872 | tf_op jit(solution)/shard_map/ppermute | solution.py:433
  3.3 2.8 %collective-permute-done = bf16[1024,256]{1,0:T(8,128)(2,1)S(1)} collective-permute-done((bf16[1024,256]{1,0:T(8,128)(2,1)S(1)}, bf16[1024,256]{1,0:T(8,128)(2,1)S(1)}, u32[]{:S(2)}, u32[]{:S(2)}) %collective-permute-start) | collective-permute-done | bytes 524320 | tf_op jit(solution)/shard_map/ppermute | solution.py:433
  6.1 0.2 maximum_select_fusion
  6.2 1.3 %collective-permute-start.1 = (bf16[1024,256]{1,0:T(8,128)(2,1)S(1)}, bf16[1024,256]{1,0:T(8,128)(2,1)S(1)}, u32[]{:S(2)}, u32[]{:S(2)}) collective-permute-start(bf16[1024,256]{1,0:T(8,128)(2,1)S(1)} %maximum_select_fusion), channel_id=1, source_target_pairs={{0,8},{4,36},{1,9},{5,37},{2,10},{6,38},{3,11},{7,39}} | collective-permute-start | bytes 1572872 | tf_op jit(solution)/shard_map/ppermute | solution.py:431
  7.6 0.7 pad_add_fusion.place_ref
  8.2 5.4 %question_block.1 = (bf16[256,1152]{1,0:T(8,128)(2,1)}, f32[8,1024]{1,0:T(8,128)}, f32[8,128]{1,0:T(8,128)}) custom-call(s32[3]{0:T(128)} %pad_add_fusion.place_ref, s32[256]{0:T(256)} %order_ref.1, bf16[256,1024]{1,0:T(8,128)(2,1)} %query_ref.2, bf16[1024,256]{1,0:T(8,128)(2,1)} %key_ref.5, bf16[1024,256]{1,0:T(8,128)(2,1)} %value_ref.5, ...), custom_call_target="tpu_custom_call" | custom-call | flops 67108864 | bytes 262144 | tf_op jit(solution)/shard_map/question_block/pallas_call | solution.py:122
  13.6 0.1 collective-permute-done.1
  13.6 0.1 add.12
  13.8 2.5 %collective-permute-start.2 = (bf16[1024,256]{1,0:T(8,128)(2,1)S(1)}, bf16[1024,256]{1,0:T(8,128)(2,1)S(1)}, u32[]{:S(2)}, u32[]{:S(2)}) collective-permute-start(bf16[1024,256]{1,0:T(8,128)(2,1)S(1)} %add.12), channel_id=1, source_target_pairs={{0,24},{8,16},{4,100},{36,68},{1,25},{9,17},{5,101},{37,69},{2,26}... | collective-permute-start | bytes 1572872 | tf_op jit(solution)/shard_map/ppermute | solution.py:431
  16.2 6.4 %context_own.2 = (f32[1024,512]{1,0:T(8,128)}, f32[1024,128]{1,0:T(8,128)}) custom-call(s32[3]{0:T(128)} %pad_add_fusion.place_ref, bf16[1024,1024]{1,0:T(8,128)(2,1)} %query_ref.5, bf16[1024,256]{1,0:T(8,128)(2,1)} %key_ref.5, bf16[1024,256]{1,0:T(8,128)(2,1)} %value_ref.5), custom_call_target="tpu_custom_call" | custom-call | flops 67108864 | bytes 262144 | tf_op jit(solution)/shard_map/context_own/pallas_call | solution.py:283
  22.7 0.0 collective-permute-done.2
  22.7 0.1 add.13
  22.8 1.3 %collective-permute-start.3 = (bf16[1024,256]{1,0:T(8,128)(2,1)S(1)}, bf16[1024,256]{1,0:T(8,128)(2,1)S(1)}, u32[]{:S(2)}, u32[]{:S(2)}) collective-permute-start(bf16[1024,256]{1,0:T(8,128)(2,1)S(1)} %add.13), channel_id=1, source_target_pairs={{0,32},{8,40},{16,48},{24,56},{4,12},{36,44},{68,76},{100,108},{1,... | collective-permute-start | bytes 1572872 | tf_op jit(solution)/shard_map/ppermute | solution.py:431
  24.2 6.4 %all-to-all-start = ((bf16[32,8,1152]{2,1,0:T(8,128)(2,1)}), bf16[32,8,1152]{2,1,0:T(8,128)(2,1)S(1)}, u32[]{:S(2)}, u32[]{:S(2)}) async-start(bf16[32,8,1152]{2,1,0:T(8,128)(2,1)} %bitcast.4), calls=%async_computation | async-start | bytes 1179648 | tf_op jit(solution)/shard_map/all_to_all | solution.py:414
  30.6 6.5 %context_own.3 = (f32[1024,512]{1,0:T(8,128)}, f32[1024,128]{1,0:T(8,128)}) custom-call(s32[3]{0:T(128)} %pad_add_fusion.place_ref, bf16[1024,1024]{1,0:T(8,128)(2,1)} %query_ref.5, bf16[1024,256]{1,0:T(8,128)(2,1)} %key_ref.5, bf16[1024,256]{1,0:T(8,128)(2,1)} %value_ref.5), custom_call_target="tpu_custom_call" | custom-call | flops 67108864 | bytes 262144 | tf_op jit(solution)/shard_map/context_own/pallas_call | solution.py:283
  37.0 0.0 collective-permute-done.3
  37.0 0.1 add.14
  37.2 4.5 %collective-permute-start.4 = (bf16[1024,256]{1,0:T(8,128)(2,1)S(1)}, bf16[1024,256]{1,0:T(8,128)(2,1)S(1)}, u32[]{:S(2)}, u32[]{:S(2)}) collective-permute-start(bf16[1024,256]{1,0:T(8,128)(2,1)S(1)} %add.14), channel_id=1, source_target_pairs={{0,96},{8,104},{16,112},{24,120},{32,64},{40,72},{48,80},{56,88},{... | collective-permute-start | bytes 1572872 | tf_op jit(solution)/shard_map/ppermute | solution.py:431
  41.7 1.1 %all-to-all-done = bf16[32,8,1152]{2,1,0:T(8,128)(2,1)S(1)} async-done(((bf16[32,8,1152]{2,1,0:T(8,128)(2,1)}), bf16[32,8,1152]{2,1,0:T(8,128)(2,1)S(1)}, u32[]{:S(2)}, u32[]{:S(2)}) %all-to-all-start) | async-done | bytes 589856 | tf_op jit(solution)/shard_map/all_to_all | solution.py:414
  42.8 0.8 %copy-done.1 = bf16[32,8,1152]{2,1,0:T(8,128)(2,1)} copy-done((bf16[32,8,1152]{2,1,0:T(8,128)(2,1)}, bf16[32,8,1152]{2,1,0:T(8,128)(2,1)S(1)}, u32[]{:S(2)}) %copy-start.1) | copy-done | bytes 589848
  43.6 4.8 %question_merge.1 = f32[4,8,1024]{2,1,0:T(8,128)} custom-call(bf16[256,1152]{1,0:T(8,128)(2,1)} %bitcast.6, f32[8,1024]{1,0:T(8,128)} %get-tuple-element.30.self_hbm, f32[8,128]{1,0:T(8,128)} %get-tuple-element.19.self_lse_hbm, bf16[1024,4096]{1,0:T(8,128)(2,1)} %weight_hbm.1), custom_call_target="tpu_custom_call" | custom-call | flops 67108864 | bytes 9437184 | tf_op jit(solution)/shard_map/question_merge/pallas_call | solution.py:211
  48.4 0.0 collective-permute-done.4
  48.4 0.1 add.15.refs_0_.refs_1_
  48.6 0.7 collective-permute-start.5
  49.3 4.4 %all-to-all-start.1 = ((f32[4,8,1024]{2,1,0:T(8,128)}), f32[4,8,1024]{2,1,0:T(8,128)S(1)}, u32[]{:S(2)}, u32[]{:S(2)}) async-start(f32[4,8,1024]{2,1,0:T(8,128)} %question_merge.1), calls=%async_computation.1 | async-start | bytes 262144 | tf_op jit(solution)/shard_map/all_to_all | solution.py:414
  53.6 0.0 collective-permute-done.5.refs_4_.refs_5_
  53.7 0.8 %copy-done.2 = bf16[1024,256]{1,0:T(8,128)(2,1)} copy-done((bf16[1024,256]{1,0:T(8,128)(2,1)}, bf16[1024,256]{1,0:T(8,128)(2,1)S(1)}, u32[]{:S(2)}) %copy-start.2) | copy-done | bytes 524312
  54.5 17.2 %context_anchor.1 = bf16[1024,1024]{1,0:T(8,128)(2,1)} custom-call(s32[3]{0:T(128)} %pad_add_fusion.place_ref, bf16[1024,1024]{1,0:T(8,128)(2,1)} %query_ref.5, bf16[1024,256]{1,0:T(8,128)(2,1)} %copy-done, bf16[1024,256]{1,0:T(8,128)(2,1)} %copy-done, f32[1024,512]{1,0:T(8,128)} %get-tuple-element.32.refs_2_, f32[1024,128]{1,0:T(8,128)} %get-tuple-element.22.refs_3_, ...), custom_call_target="tpu_custom_call" | custom-call | flops 2147483648 | bytes 1048576 | tf_op jit(solution)/shard_map/context_anchor/pallas_call | solution.py:375
  71.7 0.0 all-to-all-done.1
  71.7 0.6 reduce_sum.9
  (4 shorter events, 0.0 us)
Async XLA Ops:
  2.0 4.1 %collective-permute-start = (bf16[1024,256]{1,0:T(8,128)(2,1)S(1)}, bf16[1024,256]{1,0:T(8,128)(2,1)S(1)}, u32[]{:S(2)}, u32[]{:S(2)}) collective-permute-start(bf16[1024,256]{1,0:T(8,128)(2,1)S(1)} %pad_maximum_fusion), channel_id=1, source_target_pairs={{0,4},{1,5},{2,6},{3,7}} | collective-permute-start | bytes 1572872 | tf_op jit(solution)/shard_map/ppermute | solution.py:433
  6.2 7.4 %collective-permute-start.1 = (bf16[1024,256]{1,0:T(8,128)(2,1)S(1)}, bf16[1024,256]{1,0:T(8,128)(2,1)S(1)}, u32[]{:S(2)}, u32[]{:S(2)}) collective-permute-start(bf16[1024,256]{1,0:T(8,128)(2,1)S(1)} %maximum_select_fusion), channel_id=1, source_target_pairs={{0,8},{4,36},{1,9},{5,37},{2,10},{6,38},{3,11},{7,39}} | collective-permute-start | bytes 1572872 | tf_op jit(solution)/shard_map/ppermute | solution.py:431
  13.8 8.9 %collective-permute-start.2 = (bf16[1024,256]{1,0:T(8,128)(2,1)S(1)}, bf16[1024,256]{1,0:T(8,128)(2,1)S(1)}, u32[]{:S(2)}, u32[]{:S(2)}) collective-permute-start(bf16[1024,256]{1,0:T(8,128)(2,1)S(1)} %add.12), channel_id=1, source_target_pairs={{0,24},{8,16},{4,100},{36,68},{1,25},{9,17},{5,101},{37,69},{2,26}... | collective-permute-start | bytes 1572872 | tf_op jit(solution)/shard_map/ppermute | solution.py:431
  22.8 14.2 %collective-permute-start.3 = (bf16[1024,256]{1,0:T(8,128)(2,1)S(1)}, bf16[1024,256]{1,0:T(8,128)(2,1)S(1)}, u32[]{:S(2)}, u32[]{:S(2)}) collective-permute-start(bf16[1024,256]{1,0:T(8,128)(2,1)S(1)} %add.13), channel_id=1, source_target_pairs={{0,32},{8,40},{16,48},{24,56},{4,12},{36,44},{68,76},{100,108},{1,... | collective-permute-start | bytes 1572872 | tf_op jit(solution)/shard_map/ppermute | solution.py:431
  24.2 18.6 %all-to-all-start = ((bf16[32,8,1152]{2,1,0:T(8,128)(2,1)}), bf16[32,8,1152]{2,1,0:T(8,128)(2,1)S(1)}, u32[]{:S(2)}, u32[]{:S(2)}) async-start(bf16[32,8,1152]{2,1,0:T(8,128)(2,1)} %bitcast.4), calls=%async_computation | async-start | bytes 1179648 | tf_op jit(solution)/shard_map/all_to_all | solution.py:414
  37.2 11.2 %collective-permute-start.4 = (bf16[1024,256]{1,0:T(8,128)(2,1)S(1)}, bf16[1024,256]{1,0:T(8,128)(2,1)S(1)}, u32[]{:S(2)}, u32[]{:S(2)}) collective-permute-start(bf16[1024,256]{1,0:T(8,128)(2,1)S(1)} %add.14), channel_id=1, source_target_pairs={{0,96},{8,104},{16,112},{24,120},{32,64},{40,72},{48,80},{56,88},{... | collective-permute-start | bytes 1572872 | tf_op jit(solution)/shard_map/ppermute | solution.py:431
  42.8 0.8 %copy-start.1 = (bf16[32,8,1152]{2,1,0:T(8,128)(2,1)}, bf16[32,8,1152]{2,1,0:T(8,128)(2,1)S(1)}, u32[]{:S(2)}) copy-start(bf16[32,8,1152]{2,1,0:T(8,128)(2,1)S(1)} %all-to-all-done) | copy-start | bytes 1769476
  48.6 5.1 %copy-start = (bf16[1024,256]{1,0:T(8,128)(2,1)}, bf16[1024,256]{1,0:T(8,128)(2,1)S(1)}, u32[]{:S(2)}) copy-start(bf16[1024,256]{1,0:T(8,128)(2,1)S(1)} %add.15.refs_0_.refs_1_) | copy-start | bytes 1572868
  48.6 5.1 %collective-permute-start.5 = (bf16[1024,256]{1,0:T(8,128)(2,1)S(1)}, bf16[1024,256]{1,0:T(8,128)(2,1)S(1)}, u32[]{:S(2)}, u32[]{:S(2)}) collective-permute-start(bf16[1024,256]{1,0:T(8,128)(2,1)S(1)} %add.15.refs_0_.refs_1_), channel_id=1, source_target_pairs={{0,4},{4,0},{8,12},{12,8},{16,20},{20,16},{24,28},{28,24},{32,36},... | collective-permute-start | bytes 1572872 | tf_op jit(solution)/shard_map/ppermute | solution.py:451
  49.3 22.4 %all-to-all-start.1 = ((f32[4,8,1024]{2,1,0:T(8,128)}), f32[4,8,1024]{2,1,0:T(8,128)S(1)}, u32[]{:S(2)}, u32[]{:S(2)}) async-start(f32[4,8,1024]{2,1,0:T(8,128)} %question_merge.1), calls=%async_computation.1 | async-start | bytes 262144 | tf_op jit(solution)/shard_map/all_to_all | solution.py:414
  53.7 0.8 %copy-start.2 = (bf16[1024,256]{1,0:T(8,128)(2,1)}, bf16[1024,256]{1,0:T(8,128)(2,1)S(1)}, u32[]{:S(2)}) copy-start(bf16[1024,256]{1,0:T(8,128)(2,1)S(1)} %collective-permute-done.5.refs_4_.refs_5_) | copy-start | bytes 1572868
